TPU v7x, 32 devices: a whole 2x2x4 slice. The times are simulated.
32 devices in a mesh: clip: 2 (over y), frames: 4 (over z), rows: 2 (over x), heads: 2 (over core).
Axes of the slice: x: 2, y: 2, z: 4, core: 2. Of those that a mesh axis runs over, the one named last changes fastest.
Arguments:
- tok_q: bfloat16 [64, 32, 1536], P(('clip', 'frames'), 'rows', 'heads'), parts along dimension 0, may hold values from -125 to 125, as said below
- tok_kv: bfloat16 [2, 64, 32, 1536], P(None, ('clip', 'frames'), 'rows', 'heads'), parts along dimension 1, may hold values from -6 to 6
- ref_kv: bfloat16 [2, 4, 768, 1536], P(None, 'clip', ('frames', 'rows'), 'heads'), parts along dimension 1, may hold values from -6 to 6
- ref_ids: int32 [64], P(('clip', 'frames')), parts along dimension 0, may hold values from 0 to 1
Outputs:
- mixed: bfloat16 [64, 32, 1536], P(('clip', 'frames'), 'rows', 'heads'), parts along dimension 0
There are 2 independent parts, one for each index of `clip`. A program takes and returns all parts, laid end to end along the dimension named above; each array names one. Nothing has to cross between parts.
Inputs may be any that keep to these rules, and one draw needn't show every extreme that they name: `tok_q`: queries of the clip's tokens.
All inputs are finite; a program needn't handle non-finite values.
Results may differ from a plain program's by a relative error of at most 0.0048.
Values may be sent and summed in bfloat16 or wider, within the bound.
A program may use at most 64 MiB of HBM per device.

v0:
```python
import jax
import jax.numpy as jnp
from jax import lax
from jax.sharding import PartitionSpec as P

HEAD_DIM = 128
BAND = 8


def padded_2(value, sides, width):
    for axis, dim in sides:
        devices, length = (lax.axis_size(axis), value.shape[dim])
        up = [(i, (i + 1) % devices) for i in range(devices)]
        down = [(j, i) for i, j in up]
        last = lax.slice_in_dim(value, length - width, length, axis=dim)
        first = lax.slice_in_dim(value, 0, width, axis=dim)
        before = lax.ppermute(last, axis, up)
        after = lax.ppermute(first, axis, down)
        value = jnp.concatenate([before, value, after], axis=dim)
    return value


def attend_frame(query, frame_keys, frame_values, image_keys, image_values, factor):
    local_scores = (
        jnp.einsum("thd,shd->hts", query, frame_keys, preferred_element_type=jnp.float32) * factor
    )
    image_scores = (
        jnp.einsum("thd,shd->hts", query, image_keys, preferred_element_type=jnp.float32) * factor
    )
    top = jnp.maximum(jnp.max(local_scores, axis=-1), jnp.max(image_scores, axis=-1))
    local_exp = jnp.exp(local_scores - top[..., None])
    image_exp = jnp.exp(image_scores - top[..., None])
    total = jnp.sum(local_exp, axis=-1) + jnp.sum(image_exp, axis=-1)
    local_weights = (local_exp / total[..., None]).astype(jnp.bfloat16)
    image_weights = (image_exp / total[..., None]).astype(jnp.bfloat16)
    result = jnp.einsum(
        "hts,shd->thd", local_weights, frame_values, preferred_element_type=jnp.float32
    )
    result = result + jnp.einsum(
        "hts,shd->thd", image_weights, image_values, preferred_element_type=jnp.float32
    )
    return result


def local(tok_q, tok_kv, ref_kv, ref_ids):
    frame_count, row_count, feat_width = tok_q.shape
    head_count = feat_width // HEAD_DIM
    factor = 1.0 / HEAD_DIM**0.5
    query_heads = tok_q.reshape(frame_count, row_count, head_count, HEAD_DIM)
    padded = padded_2(tok_kv, (("frames", 1),), BAND)
    band_scores = []
    for offset in range(2 * BAND + 1):
        key_block = padded[0, offset : offset + frame_count].reshape(
            frame_count, row_count, head_count, HEAD_DIM
        )
        band_scores.append(
            jnp.einsum("frhd,frhd->frh", query_heads, key_block, preferred_element_type=jnp.float32)
            * factor
        )
    band_weights = jax.nn.softmax(jnp.stack(band_scores), axis=0).astype(jnp.bfloat16)
    temporal = jnp.zeros((frame_count, row_count, head_count, HEAD_DIM), jnp.float32)
    for offset in range(2 * BAND + 1):
        value_block = padded[1, offset : offset + frame_count].reshape(
            frame_count, row_count, head_count, HEAD_DIM
        )
        temporal = temporal + jnp.einsum(
            "frh,frhd->frhd", band_weights[offset], value_block, preferred_element_type=jnp.float32
        )
    temporal = temporal.reshape(frame_count, row_count, feat_width)
    references = lax.all_gather(ref_kv, ("frames", "rows"), axis=2, tiled=True)
    ref_length = references.shape[2]

    def spatial_frame(inputs):
        query_frame, keys_frame, values_frame, image_id = inputs
        chosen = lax.dynamic_index_in_dim(references, image_id, axis=1, keepdims=False)
        image_keys = chosen[0].reshape(ref_length, head_count, HEAD_DIM)
        image_values = chosen[1].reshape(ref_length, head_count, HEAD_DIM)
        queries = query_frame.reshape(query_frame.shape[0], head_count, HEAD_DIM)
        keys_full = keys_frame.reshape(keys_frame.shape[0], head_count, HEAD_DIM)
        values_full = values_frame.reshape(values_frame.shape[0], head_count, HEAD_DIM)
        result = attend_frame(queries, keys_full, values_full, image_keys, image_values, factor)
        return result.reshape(query_frame.shape[0], feat_width)

    query_moved, pairs_moved = (
        lax.all_to_all(tok_q[None], "rows", split_axis=1, concat_axis=2, tiled=True),
        lax.all_to_all(tok_kv, "rows", split_axis=1, concat_axis=2, tiled=True),
    )
    per_device = frame_count // lax.axis_size("rows")
    local_ids = lax.dynamic_slice_in_dim(ref_ids, lax.axis_index("rows") * per_device, per_device)
    attended = lax.map(spatial_frame, (query_moved[0], pairs_moved[0], pairs_moved[1], local_ids))
    spatial = lax.all_to_all(attended, "rows", split_axis=1, concat_axis=0, tiled=True)
    return (temporal + spatial).astype(jnp.bfloat16)


def solution(mesh):
    placed = (
        P(("clip", "frames"), "rows", "heads"),
        P(None, ("clip", "frames"), "rows", "heads"),
        P(None, "clip", ("frames", "rows"), "heads"),
        P(("clip", "frames")),
    )
    return jax.shard_map(
        local,
        mesh=mesh,
        in_specs=placed,
        out_specs=P(("clip", "frames"), "rows", "heads"),
        check_vma=False,
    )
```

profile of v0, /device:TPU:0, one launch (start us, length us, event | category | flops | bytes accessed | tf_op | source)
XLA Modules:
  0.0 203.6 jit_solution(3442192702346679367)
XLA Ops:
  6.5 2.6 %copy.150 = bf16[2,2,96,768]{3,1,0,2:T(2,128)(2,1)} copy(bf16[2,2,96,768]{3,2,1,0:T(8,128)(2,1)} %param.8) | data formatting | bytes 1179648 | tf_op args[2]
  9.1 4.2 %all-to-all-start.1 = ((bf16[1,8,16,768]{3,2,0,1:T(8,128)(2,1)}), bf16[1,8,16,768]{3,2,0,1:T(8,128)(2,1)S(1)}, u32[]{:S(2)}, u32[]{:S(2)}) async-start(bf16[1,8,16,768]{3,2,0,1:T(8,128)(2,1)} %bitcast.41), calls=%async_computation.1 | async-start | bytes 393216 | tf_op jit(solution)/shard_map/all_to_all | solution.py:85
  13.3 2.3 %collective-permute-start = (bf16[2,8,16,768]{3,2,1,0:T(8,128)(2,1)S(1)}, bf16[2,8,16,768]{3,2,1,0:T(8,128)(2,1)S(1)}, u32[]{:S(2)}, u32[]{:S(2)}) collective-permute-start(bf16[2,8,16,768]{3,2,1,0:T(8,128)(2,1)S(1)} %copy-done), channel_id=1, source_target_pairs={{0,4},{4,8},{8,12},{12,0},{1,5},{5,9},{9,13},{13,1},{2,6},{6,10},{... | collective-permute-start | bytes 1179656 | tf_op jit(solution)/shard_map/ppermute | solution.py:17
  15.7 2.1 %collective-permute-start.1 = (bf16[2,8,16,768]{3,2,1,0:T(8,128)(2,1)S(1)}, bf16[2,8,16,768]{3,2,1,0:T(8,128)(2,1)S(1)}, u32[]{:S(2)}, u32[]{:S(2)}) collective-permute-start(bf16[2,8,16,768]{3,2,1,0:T(8,128)(2,1)S(1)} %copy-done), channel_id=1, source_target_pairs={{4,0},{8,4},{12,8},{0,12},{5,1},{9,5},{13,9},{1,13},{6,2},{10,6},{... | collective-permute-start | bytes 1179656 | tf_op jit(solution)/shard_map/ppermute | solution.py:18
  17.8 1.9 reshape.210
  20.4 3.5 %all-to-all-start = ((bf16[2,8,16,768]{3,2,0,1:T(8,128)(2,1)}), bf16[2,8,16,768]{3,2,0,1:T(8,128)(2,1)S(1)}, u32[]{:S(2)}, u32[]{:S(2)}) async-start(bf16[2,8,16,768]{3,2,0,1:T(8,128)(2,1)} %copy.146), calls=%async_computation | async-start | bytes 786432 | tf_op jit(solution)/shard_map/all_to_all | solution.py:86
  26.5 7.1 %all-to-all-done = bf16[2,8,16,768]{3,2,0,1:T(8,128)(2,1)S(1)} async-done(((bf16[2,8,16,768]{3,2,0,1:T(8,128)(2,1)}), bf16[2,8,16,768]{3,2,0,1:T(8,128)(2,1)S(1)}, u32[]{:S(2)}, u32[]{:S(2)}) %all-to-all-start) | async-done | bytes 393248 | tf_op jit(solution)/shard_map/all_to_all | solution.py:86
  35.1 16.1 %collective-permute-done.1 = bf16[2,8,16,768]{3,2,1,0:T(8,128)(2,1)S(1)} collective-permute-done((bf16[2,8,16,768]{3,2,1,0:T(8,128)(2,1)S(1)}, bf16[2,8,16,768]{3,2,1,0:T(8,128)(2,1)S(1)}, u32[]{:S(2)}, u32[]{:S(2)}) %collective-permute-start.1) | collective-permute-done | bytes 393248 | tf_op jit(solution)/shard_map/ppermute | solution.py:18
  52.7 1.9 reshape_squeeze.77
  54.5 1.9 reshape_squeeze.78
  56.4 1.9 reshape_squeeze.79
  58.3 1.9 reshape_squeeze.80
  60.1 1.9 reshape_squeeze.81
  63.9 1.9 fusion.50
  65.8 1.9 reshape_squeeze.69
  67.7 1.9 reshape_squeeze.70
  69.6 1.9 reshape_squeeze.71
  78.3 5.3 %fusion.13 = (f32[8,16,6]{2,1,0:T(8,128)S(1)}, f32[8,16,6]{2,1,0:T(8,128)}, f32[8,16,6]{2,1,0:T(8,128)}, f32[8,16,6]{2,1,0:T(8,128)}, f32[8,16,6]{2,1,0:T(8,128)...) fusion(bf16[8,16,6,128]{3,2,1,0:T(8,128)(2,1)S(1)} %copy-done.1, ...), kind=kLoop, calls=%fused_computation.42 | loop fusion | flops 5098752 | bytes 3591168
  96.8 1.5 copy.130
  106.5 1.5 copy.140
  129.3 12.5 %copy.151 = bf16[2,2,768,768]{2,3,1,0:T(8,128)(2,1)} copy(bf16[2,2,768,768]{3,1,0,2:T(2,128)(2,1)} %all-gather.2.cloned.1.call-done) | data formatting | bytes 9437184 | tf_op jit(solution)/shard_map/while | solution.py:90
  141.8 44.7 %while.10 = (s32[]{:T(128)}, f32[4,32,768]{2,0,1:T(4,128)}, bf16[4,32,768]{2,1,0:T(8,128)(2,1)}, bf16[4,32,768]{2,1,0:T(8,128)(2,1)}, bf16[4,32,768]{2,1,0:T(8,1...) while((s32[]{:T(128)}, f32[4,32,768]{2,0,1:T(4,128)}, ...), condition=%wide.region_6.7_spmd, body=%wide.region_1.6_spmd.sunk | while | flops 79742592 | bytes 10604731 | solution.py:90
  144.6 1.8 constant_dynamic-slice_fusion.10
  150.1 3.0 %dynamic_update_slice.5 = f32[4,32,768]{2,0,1:T(4,128)} dynamic-update-slice(f32[4,32,768]{2,0,1:T(4,128)} %get-tuple-element.229, f32[1,32,768]{2,0,1:T(1,128)S(1)} %broadcast_in_dim.20, s32[]{:T(128)} %get-tuple-element.228, s32[]{:T(128)} %constant.11.clone.1..sunk, s32[]{:T(128)} %constant.11.clone.1..sunk) | dynamic-update-slice | bytes 196612 | tf_op jit(solution)/shard_map/while/body/jit(dynamic_update_index_in_dim)/dynamic_update_slice | solution.py:90
  155.8 1.8 constant_dynamic-slice_fusion.10
  161.2 3.0 %dynamic_update_slice.5 = f32[4,32,768]{2,0,1:T(4,128)} dynamic-update-slice(f32[4,32,768]{2,0,1:T(4,128)} %get-tuple-element.229, f32[1,32,768]{2,0,1:T(1,128)S(1)} %broadcast_in_dim.20, s32[]{:T(128)} %get-tuple-element.228, s32[]{:T(128)} %constant.11.clone.1..sunk, s32[]{:T(128)} %constant.11.clone.1..sunk) | dynamic-update-slice | bytes 196612 | tf_op jit(solution)/shard_map/while/body/jit(dynamic_update_index_in_dim)/dynamic_update_slice | solution.py:90
  167.0 1.8 constant_dynamic-slice_fusion.10
  172.4 3.0 %dynamic_update_slice.5 = f32[4,32,768]{2,0,1:T(4,128)} dynamic-update-slice(f32[4,32,768]{2,0,1:T(4,128)} %get-tuple-element.229, f32[1,32,768]{2,0,1:T(1,128)S(1)} %broadcast_in_dim.20, s32[]{:T(128)} %get-tuple-element.228, s32[]{:T(128)} %constant.11.clone.1..sunk, s32[]{:T(128)} %constant.11.clone.1..sunk) | dynamic-update-slice | bytes 196612 | tf_op jit(solution)/shard_map/while/body/jit(dynamic_update_index_in_dim)/dynamic_update_slice | solution.py:90
  178.1 1.8 constant_dynamic-slice_fusion.10
  183.6 3.0 %dynamic_update_slice.5 = f32[4,32,768]{2,0,1:T(4,128)} dynamic-update-slice(f32[4,32,768]{2,0,1:T(4,128)} %get-tuple-element.229, f32[1,32,768]{2,0,1:T(1,128)S(1)} %broadcast_in_dim.20, s32[]{:T(128)} %get-tuple-element.228, s32[]{:T(128)} %constant.11.clone.1..sunk, s32[]{:T(128)} %constant.11.clone.1..sunk) | dynamic-update-slice | bytes 196612 | tf_op jit(solution)/shard_map/while/body/jit(dynamic_update_index_in_dim)/dynamic_update_slice | solution.py:90
  186.6 3.5 %all-to-all-start.2 = ((f32[4,32,768]{2,0,1:T(4,128)}), f32[4,32,768]{2,0,1:T(4,128)S(1)}, u32[]{:S(2)}, u32[]{:S(2)}) async-start(f32[4,32,768]{2,0,1:T(4,128)} %get-tuple-element.42), calls=%async_computation.2 | async-start | bytes 786432 | tf_op jit(solution)/shard_map/all_to_all | solution.py:91
  190.1 5.6 %multiply_add_fusion = f32[8,16,6,128]{3,2,1,0:T(8,128)S(1)} fusion(f32[8,16,6,128]{3,2,1,0:T(8,128)} %reshape.262, f32[8,16,6,128]{3,2,1,0:T(8,128)} %reshape.260, f32[8,16,6,128]{3,2,1,0:T(8,128)} %reshape.258, f32[8,16,6,128]{3,2,1,0:T(8,128)} %reshape.256, f32[8,16,6,128]{3,2,1,0:T(8,128)} %reshape.254, f32[8,16,6,128]{3,2,1,0:T(8,128)} %reshape.252, ...), kind=kLoop, calls=%fused_computation.57 | loop fusion | flops 3244032 | bytes 7130112 | tf_op jit(solution)/shard_map/add | solution.py:66
  (212 shorter events, 75.5 us)
Async XLA Ops:
  6.5 6.8 %copy-start = (bf16[2,8,16,768]{3,2,1,0:T(8,128)(2,1)S(1)}, bf16[2,8,16,768]{3,2,1,0:T(8,128)(2,1)}, u32[]{:S(2)}) copy-start(bf16[2,8,16,768]{3,2,1,0:T(8,128)(2,1)} %param.7) | copy-start | bytes 1179652
  6.5 122.8 %all-gather.2.cloned.1.call-start = ((), (), s32[]{:S(2)}) async-start(), calls=%async_computation.3 | async-start | bytes 5308416 | tf_op jit(solution)/shard_map/all_gather | solution.py:70
  9.1 11.3 %all-to-all-start.1 = ((bf16[1,8,16,768]{3,2,0,1:T(8,128)(2,1)}), bf16[1,8,16,768]{3,2,0,1:T(8,128)(2,1)S(1)}, u32[]{:S(2)}, u32[]{:S(2)}) async-start(bf16[1,8,16,768]{3,2,0,1:T(8,128)(2,1)} %bitcast.41), calls=%async_computation.1 | async-start | bytes 393216 | tf_op jit(solution)/shard_map/all_to_all | solution.py:85
  13.3 21.7 %collective-permute-start = (bf16[2,8,16,768]{3,2,1,0:T(8,128)(2,1)S(1)}, bf16[2,8,16,768]{3,2,1,0:T(8,128)(2,1)S(1)}, u32[]{:S(2)}, u32[]{:S(2)}) collective-permute-start(bf16[2,8,16,768]{3,2,1,0:T(8,128)(2,1)S(1)} %copy-done), channel_id=1, source_target_pairs={{0,4},{4,8},{8,12},{12,0},{1,5},{5,9},{9,13},{13,1},{2,6},{6,10},{... | collective-permute-start | bytes 1179656 | tf_op jit(solution)/shard_map/ppermute | solution.py:17
  15.7 35.6 %collective-permute-start.1 = (bf16[2,8,16,768]{3,2,1,0:T(8,128)(2,1)S(1)}, bf16[2,8,16,768]{3,2,1,0:T(8,128)(2,1)S(1)}, u32[]{:S(2)}, u32[]{:S(2)}) collective-permute-start(bf16[2,8,16,768]{3,2,1,0:T(8,128)(2,1)S(1)} %copy-done), channel_id=1, source_target_pairs={{4,0},{8,4},{12,8},{0,12},{5,1},{9,5},{13,9},{1,13},{6,2},{10,6},{... | collective-permute-start | bytes 1179656 | tf_op jit(solution)/shard_map/ppermute | solution.py:18
  20.4 13.2 %all-to-all-start = ((bf16[2,8,16,768]{3,2,0,1:T(8,128)(2,1)}), bf16[2,8,16,768]{3,2,0,1:T(8,128)(2,1)S(1)}, u32[]{:S(2)}, u32[]{:S(2)}) async-start(bf16[2,8,16,768]{3,2,0,1:T(8,128)(2,1)} %copy.146), calls=%async_computation | async-start | bytes 786432 | tf_op jit(solution)/shard_map/all_to_all | solution.py:86
  23.9 1.8 copy-start.22
  65.8 5.7 %copy-start.14 = (bf16[1,8,16,768]{3,2,1,0:T(8,128)(2,1)S(1)}, bf16[1,8,16,768]{3,2,1,0:T(8,128)(2,1)}, u32[]{:S(2)}) copy-start(bf16[1,8,16,768]{3,2,1,0:T(8,128)(2,1)} %get-tuple-element.127) | copy-start | bytes 589828
  65.8 6.7 %copy-start.13 = (bf16[1,8,16,768]{3,2,1,0:T(8,128)(2,1)S(1)}, bf16[1,8,16,768]{3,2,1,0:T(8,128)(2,1)}, u32[]{:S(2)}) copy-start(bf16[1,8,16,768]{3,2,1,0:T(8,128)(2,1)} %get-tuple-element.126) | copy-start | bytes 589828
  75.4 2.9 %copy-start.11 = (bf16[8,16,6,128]{3,2,1,0:T(8,128)(2,1)S(1)}, bf16[8,16,6,128]{3,2,1,0:T(8,128)(2,1)}, u32[]{:S(2)}) copy-start(bf16[8,16,6,128]{3,2,1,0:T(8,128)(2,1)} %reshape.210) | copy-start | bytes 589828
  75.4 2.9 %copy-start.12 = (bf16[8,16,6,128]{3,2,1,0:T(8,128)(2,1)S(1)}, bf16[8,16,6,128]{3,2,1,0:T(8,128)(2,1)}, u32[]{:S(2)}) copy-start(bf16[8,16,6,128]{3,2,1,0:T(8,128)(2,1)} %reshape_squeeze.76) | copy-start | bytes 589828
  95.4 20.0 %copy-start.3 = (f32[1,8,16,768]{3,2,1,0:T(8,128)S(1)}, f32[1,8,16,768]{3,2,1,0:T(8,128)}, u32[]{:S(2)}) copy-start(f32[1,8,16,768]{3,2,1,0:T(8,128)} %get-tuple-element.110) | copy-start | bytes 1179652
  96.8 19.4 %copy-start.2 = (f32[1,8,16,768]{3,2,1,0:T(8,128)S(1)}, f32[1,8,16,768]{3,2,1,0:T(8,128)}, u32[]{:S(2)}) copy-start(f32[1,8,16,768]{3,2,1,0:T(8,128)} %get-tuple-element.109) | copy-start | bytes 1179652
  106.5 10.6 %copy-start.1 = (f32[1,8,16,768]{3,2,1,0:T(8,128)S(1)}, f32[1,8,16,768]{3,2,1,0:T(8,128)}, u32[]{:S(2)}) copy-start(f32[1,8,16,768]{3,2,1,0:T(8,128)} %get-tuple-element.108) | copy-start | bytes 1179652
  118.9 2.6 %copy-start.10 = (f32[1,8,16,768]{3,2,1,0:T(8,128)S(1)}, f32[1,8,16,768]{3,2,1,0:T(8,128)}, u32[]{:S(2)}) copy-start(f32[1,8,16,768]{3,2,1,0:T(8,128)} %get-tuple-element.124) | copy-start | bytes 1179652
  119.8 2.6 %copy-start.9 = (f32[1,8,16,768]{3,2,1,0:T(8,128)S(1)}, f32[1,8,16,768]{3,2,1,0:T(8,128)}, u32[]{:S(2)}) copy-start(f32[1,8,16,768]{3,2,1,0:T(8,128)} %get-tuple-element.123) | copy-start | bytes 1179652
  120.7 2.6 %copy-start.8 = (f32[1,8,16,768]{3,2,1,0:T(8,128)S(1)}, f32[1,8,16,768]{3,2,1,0:T(8,128)}, u32[]{:S(2)}) copy-start(f32[1,8,16,768]{3,2,1,0:T(8,128)} %get-tuple-element.122) | copy-start | bytes 1179652
  121.5 2.6 %copy-start.7 = (f32[1,8,16,768]{3,2,1,0:T(8,128)S(1)}, f32[1,8,16,768]{3,2,1,0:T(8,128)}, u32[]{:S(2)}) copy-start(f32[1,8,16,768]{3,2,1,0:T(8,128)} %get-tuple-element.121) | copy-start | bytes 1179652
  122.4 2.6 %copy-start.6 = (f32[1,8,16,768]{3,2,1,0:T(8,128)S(1)}, f32[1,8,16,768]{3,2,1,0:T(8,128)}, u32[]{:S(2)}) copy-start(f32[1,8,16,768]{3,2,1,0:T(8,128)} %get-tuple-element.120) | copy-start | bytes 1179652
  123.3 2.6 %copy-start.5 = (f32[1,8,16,768]{3,2,1,0:T(8,128)S(1)}, f32[1,8,16,768]{3,2,1,0:T(8,128)}, u32[]{:S(2)}) copy-start(f32[1,8,16,768]{3,2,1,0:T(8,128)} %get-tuple-element.119) | copy-start | bytes 1179652
  124.1 2.6 %copy-start.4 = (f32[1,8,16,768]{3,2,1,0:T(8,128)S(1)}, f32[1,8,16,768]{3,2,1,0:T(8,128)}, u32[]{:S(2)}) copy-start(f32[1,8,16,768]{3,2,1,0:T(8,128)} %get-tuple-element.118) | copy-start | bytes 1179652
  141.8 48.3 %copy-start.15 = (f32[8,16,6]{2,1,0:T(8,128)S(1)}, f32[8,16,6]{2,1,0:T(8,128)}, u32[]{:S(2)}) copy-start(f32[8,16,6]{2,1,0:T(8,128)} %copy.129) | copy-start | bytes 9220
  141.8 48.3 %copy-start.16 = (f32[8,16,6]{2,1,0:T(8,128)S(1)}, f32[8,16,6]{2,1,0:T(8,128)}, u32[]{:S(2)}) copy-start(f32[8,16,6]{2,1,0:T(8,128)} %copy.130) | copy-start | bytes 9220
  141.8 48.3 %copy-start.17 = (f32[8,16,6]{2,1,0:T(8,128)S(1)}, f32[8,16,6]{2,1,0:T(8,128)}, u32[]{:S(2)}) copy-start(f32[8,16,6]{2,1,0:T(8,128)} %copy.131) | copy-start | bytes 9220
  141.8 48.3 %copy-start.18 = (f32[8,16,6]{2,1,0:T(8,128)S(1)}, f32[8,16,6]{2,1,0:T(8,128)}, u32[]{:S(2)}) copy-start(f32[8,16,6]{2,1,0:T(8,128)} %copy.132) | copy-start | bytes 9220
  141.8 48.3 %copy-start.19 = (f32[8,16,6]{2,1,0:T(8,128)S(1)}, f32[8,16,6]{2,1,0:T(8,128)}, u32[]{:S(2)}) copy-start(f32[8,16,6]{2,1,0:T(8,128)} %copy.133) | copy-start | bytes 9220
  141.8 48.3 %copy-start.20 = (f32[8,16,6]{2,1,0:T(8,128)S(1)}, f32[8,16,6]{2,1,0:T(8,128)}, u32[]{:S(2)}) copy-start(f32[8,16,6]{2,1,0:T(8,128)} %copy.134) | copy-start | bytes 9220
  141.8 48.3 %copy-start.21 = (f32[8,16,6]{2,1,0:T(8,128)S(1)}, f32[8,16,6]{2,1,0:T(8,128)}, u32[]{:S(2)}) copy-start(f32[8,16,6]{2,1,0:T(8,128)} %copy.135) | copy-start | bytes 9220
  186.6 9.3 %all-to-all-start.2 = ((f32[4,32,768]{2,0,1:T(4,128)}), f32[4,32,768]{2,0,1:T(4,128)S(1)}, u32[]{:S(2)}, u32[]{:S(2)}) async-start(f32[4,32,768]{2,0,1:T(4,128)} %get-tuple-element.42), calls=%async_computation.2 | async-start | bytes 786432 | tf_op jit(solution)/shard_map/all_to_all | solution.py:91
Sparse Core Ops, SparseCore 0:
  9.5 93.9 all-gather.1
where the time goes:
time: 206 us; the launch traced here: 204 us
  local copies, waits for them, and re-layouts  119 us (58%)
  waiting for transfers between devices  23.3 us (11%)
  other arithmetic  17.9 us (9%)
  starting transfers between devices  15.6 us (8%)
  between operations  13.8 us (7%)
  loops' own time  8.6 us (4%)
  matrix products  5.13 us (2%)
    another operation x17, local copies, waits for them, and re-layouts, local(): padded[0, offset:offset + frame_count]  23.8 us
    another operation x17, local copies, waits for them, and re-layouts  19.3 us
    ppermute x1, waiting for transfers between devices, padded_2(): after = lax.ppermute(first, axis, down)  16.1 us
    dot_general x17, local copies, waits for them, and re-layouts, local(): jnp.einsum('frh,frhd->frhd', band_weights[offset], value_block, preferred...  14.7 us
    while x1, local copies, waits for them, and re-layouts, local(): lax.map(spatial_frame, (query_moved[0], pairs_moved[0], pairs_moved[1], l...  12.5 us
    dynamic_update_slice x4, local copies, waits for them, and re-layouts, local(): lax.map(spatial_frame, (query_moved[0], pairs_moved[0], pairs_moved[1], l...  11.9 us
    dot_general x17, local copies, waits for them, and re-layouts, local(): jnp.einsum('frhd,frhd->frh', query_heads, key_block, preferred_element_ty...  11.4 us
    dynamic_slice x12, local copies, waits for them, and re-layouts, local(): lax.map(spatial_frame, (query_moved[0], pairs_moved[0], pairs_moved[1], l...  9.24 us
  transfers between devices with their start and end apart: 6, of which 2 were waited for; matrix products, arithmetic and copies ran while one was open for 44% of the time, Pallas kernels for 0%

commit v1 on v0

--- a/solution.py
+++ b/solution.py
@@ -1,6 +1,10 @@
+import functools
+
 import jax
 import jax.numpy as jnp
 from jax import lax
+from jax.experimental import pallas as pl
+from jax.experimental.pallas import tpu as pltpu
 from jax.sharding import PartitionSpec as P
 
 HEAD_DIM = 128
@@ -42,7 +46,7 @@
     return result
 
 
-def local(tok_q, tok_kv, ref_kv, ref_ids):
+def local_general(tok_q, tok_kv, ref_kv, ref_ids):
     frame_count, row_count, feat_width = tok_q.shape
     head_count = feat_width // HEAD_DIM
     factor = 1.0 / HEAD_DIM**0.5
@@ -92,6 +96,325 @@
     return (temporal + spatial).astype(jnp.bfloat16)
 
 
+NEG = -1e30
+MESH = pl.DeviceIdType.MESH
+
+
+def scores_of(keys, queries):
+    return lax.dot_general(
+        keys, queries, (((1,), (1,)), ((), ())), preferred_element_type=jnp.float32
+    )
+
+
+def kernel(
+    n,
+    q_hbm,
+    kv_hbm,
+    ref_hbm,
+    ids_ref,
+    out_ref,
+    qbuf,
+    kvbuf,
+    rbuf,
+    idbuf,
+    pref,
+    ptime,
+    pframe,
+    stats,
+    vt,
+    own,
+    part,
+    got,
+    local_sem,
+    xs_sem,
+    xr_sem,
+    qs_sem,
+    qr_sem,
+    is_sem,
+    ir_sem,
+    ss_sem,
+    sr_sem,
+    ps_sem,
+    pr_sem,
+):
+    frame_count, row_count, width = q_hbm.shape
+    head_count = width // HEAD_DIM
+    tokens = frame_count * row_count
+    images, ref_rows = ref_hbm.shape[1], ref_hbm.shape[2]
+    span = 2 * ref_rows
+    factor = 1.0 / HEAD_DIM**0.5
+    me = lax.axis_index("frames")
+    across = {"rows": 1 - lax.axis_index("rows")}
+    ahead = [{"frames": lax.rem(me + d, n)} for d in range(n)]
+    behind = [{"frames": lax.rem(me + n - d, n)} for d in range(n)]
+    banded = (0, 1, n - 1)
+    order = [0, 1, n - 1] + list(range(2, n - 1))
+
+    loads = [
+        pltpu.make_async_copy(q_hbm, qbuf.at[0], local_sem.at[0]),
+        pltpu.make_async_copy(ref_hbm.at[0], rbuf.at[0, :, pl.ds(0, ref_rows)], local_sem.at[1]),
+        pltpu.make_async_copy(kv_hbm, kvbuf.at[0], local_sem.at[2]),
+        pltpu.make_async_copy(ref_hbm.at[1], rbuf.at[1, :, pl.ds(0, ref_rows)], local_sem.at[3]),
+    ]
+    for copy in loads:
+        copy.start()
+
+    barrier = pltpu.get_barrier_semaphore()
+    for d in range(1, n):
+        pl.semaphore_signal(barrier, inc=1, device_id=ahead[d], device_id_type=MESH)
+    pl.semaphore_signal(barrier, inc=1, device_id=across, device_id_type=MESH)
+
+    lane_frame = lax.broadcasted_iota(jnp.int32, (8, tokens), 1) // row_count
+    which = jnp.zeros((8, tokens), jnp.int32)
+    for f in range(frame_count):
+        which = jnp.where(lane_frame == f, ids_ref[f], which)
+    idbuf[0] = which
+
+    pl.semaphore_wait(barrier, n)
+
+    def remote(src, dst, send, recv, where):
+        return pltpu.make_async_remote_copy(
+            src_ref=src, dst_ref=dst, send_sem=send, recv_sem=recv,
+            device_id=where, device_id_type=MESH,
+        )
+
+    far = pl.ds(ref_rows, ref_rows)
+    xcopies = [
+        remote(ref_hbm.at[0], rbuf.at[0, :, far], xs_sem.at[0], xr_sem.at[0], across),
+        remote(kv_hbm.at[0], kvbuf.at[1, 0], xs_sem.at[1], xr_sem.at[1], across),
+        remote(ref_hbm.at[1], rbuf.at[1, :, far], xs_sem.at[2], xr_sem.at[2], across),
+        remote(kv_hbm.at[1], kvbuf.at[1, 1], xs_sem.at[3], xr_sem.at[3], across),
+    ]
+    qcopies = [None] + [
+        remote(q_hbm, qbuf.at[d], qs_sem.at[d], qr_sem.at[d], ahead[d]) for d in range(1, n)
+    ]
+    icopies = [None] + [
+        remote(idbuf.at[0], idbuf.at[d], is_sem.at[d], ir_sem.at[d], ahead[d]) for d in range(1, n)
+    ]
+    for copy in icopies[1:]:
+        copy.start()
+    xcopies[0].start()
+    for d in order[1:]:
+        qcopies[d].start()
+    for copy in xcopies[1:]:
+        copy.start()
+
+    def lanes(h):
+        return pl.ds(pl.multiple_of(h * HEAD_DIM, HEAD_DIM), HEAD_DIM)
+
+    row = lax.broadcasted_iota(jnp.int32, (tokens, tokens), 0)
+    col = lax.broadcasted_iota(jnp.int32, (tokens, tokens), 1)
+    key_frame, key_row = row // row_count, row % row_count
+    query_frame, query_row = col // row_count, col % row_count
+    same_frame = key_frame == query_frame
+
+    def in_band(d):
+        mask = key_row == query_row
+        if d == 1:
+            mask = mask & (key_frame <= query_frame)
+        elif d == n - 1:
+            mask = mask & (key_frame >= query_frame)
+        return mask
+
+    def score_block(d):
+        mask = in_band(d) if d in banded else None
+
+        def body(h):
+            cut = lanes(h)
+            query = qbuf[d, :, :, cut].reshape(tokens, HEAD_DIM)
+            image_keys = rbuf[0, :, :, cut].reshape(images * span, HEAD_DIM)
+            both = scores_of(image_keys, query)
+            chosen = idbuf[d][0:1]
+            score = both[0:span]
+            for i in range(1, images):
+                score = jnp.where(chosen == i, both[i * span : (i + 1) * span], score)
+            score = score * factor
+            top = jnp.max(score, axis=0, keepdims=True)
+            zero = jnp.zeros_like(top)
+            time_top, time_sum = zero, zero
+            if d in banded:
+                keys = kvbuf[0, 0, :, :, cut].reshape(tokens, HEAD_DIM)
+                near = scores_of(keys, query) * factor
+                time_score = jnp.where(mask, near, NEG)
+                time_top = jnp.max(time_score, axis=0, keepdims=True)
+                time_exp = jnp.exp(time_score - time_top)
+                time_sum = jnp.sum(time_exp, axis=0, keepdims=True)
+                ptime[d, h] = time_exp
+            if d == 0:
+                other_keys = kvbuf[1, 0, :, :, cut].reshape(tokens, HEAD_DIM)
+                other = scores_of(other_keys, query) * factor
+                near = jnp.where(same_frame, near, NEG)
+                other = jnp.where(same_frame, other, NEG)
+                top = jnp.maximum(top, jnp.max(near, axis=0, keepdims=True))
+                top = jnp.maximum(top, jnp.max(other, axis=0, keepdims=True))
+                near = jnp.exp(near - top)
+                other = jnp.exp(other - top)
+                pframe[h, 0] = near
+                pframe[h, 1] = other
+            score = jnp.exp(score - top)
+            total = jnp.sum(score, axis=0, keepdims=True)
+            if d == 0:
+                total = total + jnp.sum(near, axis=0, keepdims=True)
+                total = total + jnp.sum(other, axis=0, keepdims=True)
+            pref[d, h] = score
+            stats[0, d, h] = jnp.concatenate([top, total, time_top, time_sum], axis=0)
+
+        return body
+
+    def each_head(body):
+        def pair(i, carry):
+            body(2 * i)
+            body(2 * i + 1)
+            return carry
+
+        lax.fori_loop(0, head_count // 2, pair, 0)
+
+    def scale_of(d, h, k):
+        tops, sums = [], []
+        for e in range(n):
+            place = (d - e) % n
+            if k == 2 and place not in banded:
+                continue
+            block = stats[e, place, h]
+            tops.append(block[k : k + 1])
+            sums.append(block[k + 1 : k + 2])
+        top = functools.reduce(jnp.maximum, tops)
+        total = sum(s * jnp.exp(t - top) for t, s in zip(tops, sums))
+        return jnp.exp(tops[0] - top) / total
+
+    def value_block(d):
+        def body(h):
+            chosen = idbuf[d][0:1]
+            weight = pref[d, h] * scale_of(d, h, 0)
+            weights = [
+                jnp.where(chosen == i, weight, 0.0).astype(jnp.bfloat16) for i in range(images)
+            ]
+            if d in banded:
+                weights.append((ptime[d, h] * scale_of(d, h, 2)).astype(jnp.bfloat16))
+            weight = jnp.concatenate(weights, axis=0)
+            values = vt[h, :, 0 : weight.shape[0]]
+            result = jnp.dot(values, weight, preferred_element_type=jnp.float32)
+            if d == 0:
+                scale = scale_of(d, h, 0)
+                for i in range(2):
+                    start = images * span + i * tokens
+                    result = result + jnp.dot(
+                        vt[h, :, start : start + tokens],
+                        (pframe[h, i] * scale).astype(jnp.bfloat16),
+                        preferred_element_type=jnp.float32,
+                    )
+                own[h] = result
+            else:
+                part[d, h] = result.astype(jnp.bfloat16)
+
+        return body
+
+    def turn_values(h):
+        cut = lanes(h)
+        blocks = [
+            rbuf[1, :, :, cut].reshape(images * span, HEAD_DIM),
+            kvbuf[0, 1, :, :, cut].reshape(tokens, HEAD_DIM),
+            kvbuf[1, 1, :, :, cut].reshape(tokens, HEAD_DIM),
+        ]
+        values = jnp.concatenate(blocks, axis=0).astype(jnp.float32)
+        vt[h] = values.T.astype(jnp.bfloat16)
+
+    for copy in loads:
+        copy.wait()
+    xcopies[0].wait_recv()
+    xcopies[1].wait_recv()
+    each_head(score_block(0))
+    for d in order[1:]:
+        icopies[d].wait_recv()
+        qcopies[d].wait_recv()
+        each_head(score_block(d))
+    scopies = [None] + [
+        remote(stats.at[0], stats.at[d], ss_sem.at[d], sr_sem.at[d], ahead[d])
+        for d in range(1, n)
+    ]
+    for copy in scopies[1:]:
+        copy.start()
+    xcopies[2].wait_recv()
+    xcopies[3].wait_recv()
+    each_head(turn_values)
+    for copy in scopies[1:]:
+        copy.wait_recv()
+    pcopies = [None] + [
+        remote(part.at[d], got.at[d], ps_sem.at[d], pr_sem.at[d], behind[d]) for d in range(1, n)
+    ]
+    for d in order[:0:-1]:
+        each_head(value_block(d))
+        pcopies[d].start()
+    each_head(value_block(0))
+    for copy in pcopies[1:]:
+        copy.wait_recv()
+
+    def finish(h):
+        total = own[h]
+        for d in range(1, n):
+            total = total + got[d, h].astype(jnp.float32)
+        out_ref[:, :, lanes(h)] = total.T.reshape(frame_count, row_count, HEAD_DIM).astype(
+            jnp.bfloat16
+        )
+
+    each_head(finish)
+    for copies in (xcopies, qcopies[1:], icopies[1:], scopies[1:], pcopies[1:]):
+        for copy in copies:
+            copy.wait_send()
+
+
+def local_kernel(tok_q, tok_kv, ref_kv, ref_ids):
+    n = lax.axis_size("frames")
+    frame_count, row_count, width = tok_q.shape
+    heads = width // HEAD_DIM
+    tokens = frame_count * row_count
+    images, ref_rows = ref_kv.shape[1:3]
+    span = 2 * ref_rows
+    dma = pltpu.SemaphoreType.DMA
+    anywhere = pl.BlockSpec(memory_space=pl.ANY)
+    return pl.pallas_call(
+        functools.partial(kernel, n),
+        out_shape=jax.ShapeDtypeStruct(tok_q.shape, jnp.bfloat16),
+        in_specs=[anywhere] * 3 + [pl.BlockSpec(memory_space=pltpu.SMEM)],
+        out_specs=pl.BlockSpec(memory_space=pltpu.VMEM),
+        scratch_shapes=[
+            pltpu.VMEM((n,) + tok_q.shape, jnp.bfloat16),
+            pltpu.VMEM((2,) + tok_kv.shape, jnp.bfloat16),
+            pltpu.VMEM((2, images, span, width), jnp.bfloat16),
+            pltpu.VMEM((n, 8, tokens), jnp.int32),
+            pltpu.VMEM((n, heads, span, tokens), jnp.float32),
+            pltpu.VMEM((n, heads, tokens, tokens), jnp.float32),
+            pltpu.VMEM((heads, 2, tokens, tokens), jnp.float32),
+            pltpu.VMEM((n, n, heads, 4, tokens), jnp.float32),
+            pltpu.VMEM((heads, HEAD_DIM, images * span + 2 * tokens), jnp.bfloat16),
+            pltpu.VMEM((heads, HEAD_DIM, tokens), jnp.float32),
+            pltpu.VMEM((n, heads, HEAD_DIM, tokens), jnp.bfloat16),
+            pltpu.VMEM((n, heads, HEAD_DIM, tokens), jnp.bfloat16),
+            dma((4,)),
+            dma((4,)),
+            dma((4,)),
+        ]
+        + [dma((n,))] * 8,
+        compiler_params=pltpu.CompilerParams(
+            collective_id=0, has_side_effects=True, vmem_limit_bytes=48 * 1024 * 1024
+        ),
+    )(tok_q, tok_kv, ref_kv, ref_ids)
+
+
+def local(tok_q, tok_kv, ref_kv, ref_ids):
+    frame_count, row_count, width = tok_q.shape
+    fits = (
+        3 <= lax.axis_size("frames") <= 8
+        and lax.axis_size("rows") == 2
+        and frame_count == BAND
+        and row_count % 16 == 0
+        and frame_count * row_count == 128
+        and ref_kv.shape[2] % 16 == 0
+        and (width // HEAD_DIM) % 2 == 0
+    )
+    return (local_kernel if fits else local_general)(tok_q, tok_kv, ref_kv, ref_ids)
+
+
 def solution(mesh):
     placed = (
         P(("clip", "frames"), "rows", "heads"),

time: 206 us -> 51.4 us (0.25)
  the two profiles are of different devices: /device:TPU:0 before, /device:TPU:10 now
where the time goes in v1:
time: 51.4 us; the launch traced here: 51.1 us
  Pallas kernels  46.8 us (91%)
  local copies, waits for them, and re-layouts  4.32 us (8%)
    pallas_call x1, Pallas kernels, local_kernel(): pl.pallas_call(functools.partial(kernel, n), out_shape=jax.ShapeDtypeStru...  46.8 us
    unnamed x9, local copies, waits for them, and re-layouts  4.32 us

profile of v1, /device:TPU:10, one launch (start us, length us, event | category | flops | bytes accessed | tf_op | source)
XLA Modules:
  0.0 51.1 jit_solution(12929873879543445145)
XLA Ops:
  0.0 0.0 copy-start
  0.0 1.1 %copy-done = bf16[2,2,96,768]{3,2,1,0:T(8,128)(2,1)S(1)} copy-done((bf16[2,2,96,768]{3,2,1,0:T(8,128)(2,1)S(1)}, bf16[2,2,96,768]{3,2,1,0:T(8,128)(2,1)}, u32[]{:S(2)}) %copy-start) | copy-done | bytes 589848
  1.1 0.0 copy-start.1
  1.1 1.0 %copy-done.1 = bf16[2,8,16,768]{3,2,1,0:T(8,128)(2,1)S(1)} copy-done((bf16[2,8,16,768]{3,2,1,0:T(8,128)(2,1)S(1)}, bf16[2,8,16,768]{3,2,1,0:T(8,128)(2,1)}, u32[]{:S(2)}) %copy-start.1) | copy-done | bytes 393240
  2.1 0.0 copy-start.2
  2.1 0.9 %copy-done.2 = bf16[8,16,768]{2,1,0:T(8,128)(2,1)S(1)} copy-done((bf16[8,16,768]{2,1,0:T(8,128)(2,1)S(1)}, bf16[8,16,768]{2,1,0:T(8,128)(2,1)}, u32[]{:S(2)}) %copy-start.2) | copy-done | bytes 196632
  3.0 0.0 copy-start.3
  3.0 0.7 %copy-done.3 = s32[8]{0:T(128)S(1)} copy-done((s32[8]{0:T(128)S(1)}, s32[8]{0:T(128)}, u32[]{:S(2)}) %copy-start.3) | copy-done | bytes 56
  3.6 46.8 %shard_map.46 = bf16[8,16,768]{2,1,0:T(8,128)(2,1)S(1)} custom-call(bf16[8,16,768]{2,1,0:T(8,128)(2,1)S(1)} %copy-done.2, bf16[2,8,16,768]{3,2,1,0:T(8,128)(2,1)S(1)} %copy-done.1, bf16[2,2,96,768]{3,2,1,0:T(8,128)(2,1)S(1)} %copy-done, s32[8]{0:T(128)S(1)} %copy-done.3), custom_call_target="tpu_custom_call" | custom-call | tf_op jit(solution)/shard_map/pallas_call | solution.py:375
  50.5 0.7 %copy.6 = bf16[8,16,768]{2,1,0:T(8,128)(2,1)} copy(bf16[8,16,768]{2,1,0:T(8,128)(2,1)S(1)} %shard_map.46) | data formatting | bytes 393216
Async XLA Ops:
  0.0 1.1 %copy-start = (bf16[2,2,96,768]{3,2,1,0:T(8,128)(2,1)S(1)}, bf16[2,2,96,768]{3,2,1,0:T(8,128)(2,1)}, u32[]{:S(2)}) copy-start(bf16[2,2,96,768]{3,2,1,0:T(8,128)(2,1)} %ref_hbm.1) | copy-start | bytes 1769476
  1.1 1.0 %copy-start.1 = (bf16[2,8,16,768]{3,2,1,0:T(8,128)(2,1)S(1)}, bf16[2,8,16,768]{3,2,1,0:T(8,128)(2,1)}, u32[]{:S(2)}) copy-start(bf16[2,8,16,768]{3,2,1,0:T(8,128)(2,1)} %kv_hbm.1) | copy-start | bytes 1179652
  2.1 0.9 %copy-start.2 = (bf16[8,16,768]{2,1,0:T(8,128)(2,1)S(1)}, bf16[8,16,768]{2,1,0:T(8,128)(2,1)}, u32[]{:S(2)}) copy-start(bf16[8,16,768]{2,1,0:T(8,128)(2,1)} %q_hbm.1) | copy-start | bytes 589828
  3.0 0.7 %copy-start.3 = (s32[8]{0:T(128)S(1)}, s32[8]{0:T(128)}, u32[]{:S(2)}) copy-start(s32[8]{0:T(128)} %ids_ref.1) | copy-start | bytes 100

commit v2 on v1

--- a/solution.py
+++ b/solution.py
@@ -108,6 +108,7 @@
 
 def kernel(
     n,
+    chunks,
     q_hbm,
     kv_hbm,
     ref_hbm,
@@ -122,7 +123,7 @@
     pframe,
     stats,
     vt,
-    own,
+    mine,
     part,
     got,
     local_sem,
@@ -139,22 +140,27 @@
 ):
     frame_count, row_count, width = q_hbm.shape
     head_count = width // HEAD_DIM
+    per_chunk = head_count // chunks
+    chunk_width = per_chunk * HEAD_DIM
     tokens = frame_count * row_count
     images, ref_rows = ref_hbm.shape[1], ref_hbm.shape[2]
     span = 2 * ref_rows
     factor = 1.0 / HEAD_DIM**0.5
     me = lax.axis_index("frames")
+    has_left, has_right = me >= 1, me <= n - 2
+    middle = has_left & has_right
     across = {"rows": 1 - lax.axis_index("rows")}
     ahead = [{"frames": lax.rem(me + d, n)} for d in range(n)]
-    behind = [{"frames": lax.rem(me + n - d, n)} for d in range(n)]
+    right, left = ahead[1], ahead[n - 1]
     banded = (0, 1, n - 1)
-    order = [0, 1, n - 1] + list(range(2, n - 1))
+    far_slots = list(range(2, n - 1))
+    own_rows, far_rows = pl.ds(0, ref_rows), pl.ds(ref_rows, ref_rows)
 
     loads = [
         pltpu.make_async_copy(q_hbm, qbuf.at[0], local_sem.at[0]),
-        pltpu.make_async_copy(ref_hbm.at[0], rbuf.at[0, :, pl.ds(0, ref_rows)], local_sem.at[1]),
+        pltpu.make_async_copy(ref_hbm.at[0], rbuf.at[0, :, own_rows], local_sem.at[1]),
         pltpu.make_async_copy(kv_hbm, kvbuf.at[0], local_sem.at[2]),
-        pltpu.make_async_copy(ref_hbm.at[1], rbuf.at[1, :, pl.ds(0, ref_rows)], local_sem.at[3]),
+        pltpu.make_async_copy(ref_hbm.at[1], rbuf.at[1, :, own_rows], local_sem.at[3]),
     ]
     for copy in loads:
         copy.start()
@@ -178,35 +184,66 @@
             device_id=where, device_id_type=MESH,
         )
 
-    far = pl.ds(ref_rows, ref_rows)
-    xcopies = [
-        remote(ref_hbm.at[0], rbuf.at[0, :, far], xs_sem.at[0], xr_sem.at[0], across),
-        remote(kv_hbm.at[0], kvbuf.at[1, 0], xs_sem.at[1], xr_sem.at[1], across),
-        remote(ref_hbm.at[1], rbuf.at[1, :, far], xs_sem.at[2], xr_sem.at[2], across),
-        remote(kv_hbm.at[1], kvbuf.at[1, 1], xs_sem.at[3], xr_sem.at[3], across),
-    ]
-    qcopies = [None] + [
-        remote(q_hbm, qbuf.at[d], qs_sem.at[d], qr_sem.at[d], ahead[d]) for d in range(1, n)
-    ]
+    def part_of(c):
+        return pl.ds(c * chunk_width, chunk_width)
+
+    def x_copy(c, k):
+        cut = part_of(c)
+        if k % 2 == 0:
+            src, dst = ref_hbm.at[k // 2, :, :, cut], rbuf.at[k // 2, :, far_rows, cut]
+        else:
+            src, dst = kv_hbm.at[k // 2, :, :, cut], kvbuf.at[1, k // 2, :, :, cut]
+        return remote(src, dst, xs_sem.at[c, k], xr_sem.at[c, k], across)
+
+    def q_right(c, d):
+        cut = part_of(c)
+        src = q_hbm.at[:, :, cut] if d == 0 else qbuf.at[d, :, :, cut]
+        return remote(
+            src, qbuf.at[d + 1, :, :, cut], qs_sem.at[c, d], qr_sem.at[c, d + 1], right
+        )
+
+    def q_left(c, d):
+        cut = part_of(c)
+        src = q_hbm.at[:, :, cut] if d == 0 else qbuf.at[d, :, :, cut]
+        to = (d if d else n) - 1
+        return remote(
+            src, qbuf.at[to, :, :, cut], qs_sem.at[c, d if d else n], qr_sem.at[c, to], left
+        )
+
+    def q_moves(d):
+        if d == 0:
+            return [(has_right, q_right), (has_left, q_left)]
+        moves = []
+        if d < n - 1:
+            moves.append(((d <= me) & has_right, q_right))
+        if d > 1:
+            moves.append(((d > me) & has_left, q_left))
+        return moves
+
+    def send_queries(c, d):
+        for flag, make in q_moves(d):
+            pl.when(flag)(lambda make=make: make(c, d).start())
+
+    def take_queries(c, d):
+        cut = part_of(c)
+        held = qbuf.at[d, :, :, cut]
+        remote(held, held, qs_sem.at[c, d], qr_sem.at[c, d], right).wait_recv()
+        send_queries(c, d)
+
     icopies = [None] + [
         remote(idbuf.at[0], idbuf.at[d], is_sem.at[d], ir_sem.at[d], ahead[d]) for d in range(1, n)
     ]
     for copy in icopies[1:]:
         copy.start()
-    xcopies[0].start()
-    for d in order[1:]:
-        qcopies[d].start()
-    for copy in xcopies[1:]:
-        copy.start()
-
-    def lanes(h):
-        return pl.ds(pl.multiple_of(h * HEAD_DIM, HEAD_DIM), HEAD_DIM)
+    for c in range(chunks):
+        send_queries(c, 0)
+        for k in range(4):
+            x_copy(c, k).start()
 
     row = lax.broadcasted_iota(jnp.int32, (tokens, tokens), 0)
     col = lax.broadcasted_iota(jnp.int32, (tokens, tokens), 1)
     key_frame, key_row = row // row_count, row % row_count
     query_frame, query_row = col // row_count, col % row_count
-    same_frame = key_frame == query_frame
 
     def in_band(d):
         mask = key_row == query_row
@@ -216,11 +253,11 @@
             mask = mask & (key_frame >= query_frame)
         return mask
 
-    def score_block(d):
-        mask = in_band(d) if d in banded else None
-
-        def body(h):
-            cut = lanes(h)
+    def heads_of(c):
+        return [(h, pl.ds(h * HEAD_DIM, HEAD_DIM)) for h in range(c * per_chunk, (c + 1) * per_chunk)]
+
+    def score_block(c, d):
+        for h, cut in heads_of(c):
             query = qbuf[d, :, :, cut].reshape(tokens, HEAD_DIM)
             image_keys = rbuf[0, :, :, cut].reshape(images * span, HEAD_DIM)
             both = scores_of(image_keys, query)
@@ -230,12 +267,11 @@
                 score = jnp.where(chosen == i, both[i * span : (i + 1) * span], score)
             score = score * factor
             top = jnp.max(score, axis=0, keepdims=True)
-            zero = jnp.zeros_like(top)
-            time_top, time_sum = zero, zero
+            time_top, time_sum = jnp.zeros_like(top), jnp.zeros_like(top)
             if d in banded:
                 keys = kvbuf[0, 0, :, :, cut].reshape(tokens, HEAD_DIM)
                 near = scores_of(keys, query) * factor
-                time_score = jnp.where(mask, near, NEG)
+                time_score = jnp.where(in_band(d), near, NEG)
                 time_top = jnp.max(time_score, axis=0, keepdims=True)
                 time_exp = jnp.exp(time_score - time_top)
                 time_sum = jnp.sum(time_exp, axis=0, keepdims=True)
@@ -243,8 +279,8 @@
             if d == 0:
                 other_keys = kvbuf[1, 0, :, :, cut].reshape(tokens, HEAD_DIM)
                 other = scores_of(other_keys, query) * factor
-                near = jnp.where(same_frame, near, NEG)
-                other = jnp.where(same_frame, other, NEG)
+                near = jnp.where(key_frame == query_frame, near, NEG)
+                other = jnp.where(key_frame == query_frame, other, NEG)
                 top = jnp.maximum(top, jnp.max(near, axis=0, keepdims=True))
                 top = jnp.maximum(top, jnp.max(other, axis=0, keepdims=True))
                 near = jnp.exp(near - top)
@@ -257,45 +293,37 @@
                 total = total + jnp.sum(near, axis=0, keepdims=True)
                 total = total + jnp.sum(other, axis=0, keepdims=True)
             pref[d, h] = score
-            stats[0, d, h] = jnp.concatenate([top, total, time_top, time_sum], axis=0)
-
-        return body
-
-    def each_head(body):
-        def pair(i, carry):
-            body(2 * i)
-            body(2 * i + 1)
-            return carry
-
-        lax.fori_loop(0, head_count // 2, pair, 0)
-
-    def scale_of(d, h, k):
+            stats[0, c, d, h % per_chunk] = jnp.concatenate(
+                [top, total, time_top, time_sum], axis=0
+            )
+
+    def scale_of(c, d, h, k):
         tops, sums = [], []
         for e in range(n):
             place = (d - e) % n
             if k == 2 and place not in banded:
                 continue
-            block = stats[e, place, h]
+            block = stats[e, c, place, h % per_chunk]
             tops.append(block[k : k + 1])
             sums.append(block[k + 1 : k + 2])
         top = functools.reduce(jnp.maximum, tops)
         total = sum(s * jnp.exp(t - top) for t, s in zip(tops, sums))
         return jnp.exp(tops[0] - top) / total
 
-    def value_block(d):
-        def body(h):
+    def value_block(c, d):
+        for h, cut in heads_of(c):
             chosen = idbuf[d][0:1]
-            weight = pref[d, h] * scale_of(d, h, 0)
+            scale = scale_of(c, d, h, 0)
+            weight = pref[d, h] * scale
             weights = [
                 jnp.where(chosen == i, weight, 0.0).astype(jnp.bfloat16) for i in range(images)
             ]
             if d in banded:
-                weights.append((ptime[d, h] * scale_of(d, h, 2)).astype(jnp.bfloat16))
+                weights.append((ptime[d, h] * scale_of(c, d, h, 2)).astype(jnp.bfloat16))
             weight = jnp.concatenate(weights, axis=0)
             values = vt[h, :, 0 : weight.shape[0]]
             result = jnp.dot(values, weight, preferred_element_type=jnp.float32)
             if d == 0:
-                scale = scale_of(d, h, 0)
                 for i in range(2):
                     start = images * span + i * tokens
                     result = result + jnp.dot(
@@ -303,79 +331,149 @@
                         (pframe[h, i] * scale).astype(jnp.bfloat16),
                         preferred_element_type=jnp.float32,
                     )
-                own[h] = result
-            else:
-                part[d, h] = result.astype(jnp.bfloat16)
-
-        return body
-
-    def turn_values(h):
-        cut = lanes(h)
-        blocks = [
-            rbuf[1, :, :, cut].reshape(images * span, HEAD_DIM),
-            kvbuf[0, 1, :, :, cut].reshape(tokens, HEAD_DIM),
-            kvbuf[1, 1, :, :, cut].reshape(tokens, HEAD_DIM),
-        ]
-        values = jnp.concatenate(blocks, axis=0).astype(jnp.float32)
-        vt[h] = values.T.astype(jnp.bfloat16)
-
+            mine[d, h] = result
+
+    def turn_values(c):
+        for h, cut in heads_of(c):
+            blocks = [
+                rbuf[1, :, :, cut].reshape(images * span, HEAD_DIM),
+                kvbuf[0, 1, :, :, cut].reshape(tokens, HEAD_DIM),
+                kvbuf[1, 1, :, :, cut].reshape(tokens, HEAD_DIM),
+            ]
+            values = jnp.concatenate(blocks, axis=0).astype(jnp.float32)
+            vt[h] = values.T.astype(jnp.bfloat16)
+
+    def stats_copy(c, d):
+        return remote(stats.at[0, c], stats.at[d, c], ss_sem.at[c, d], sr_sem.at[c, d], ahead[d])
+
+    def p_left(c, d):
+        held = pl.ds(c * per_chunk, per_chunk)
+        return remote(
+            part.at[d, held], got.at[d - 1, held], ps_sem.at[c, d], pr_sem.at[c, d - 1], left
+        )
+
+    def p_right(c, d):
+        held = pl.ds(c * per_chunk, per_chunk)
+        return remote(
+            part.at[d, held], got.at[d + 1, held], ps_sem.at[c, d], pr_sem.at[c, d + 1], right
+        )
+
+    def p_wait(c, d):
+        held = got.at[d, pl.ds(c * per_chunk, per_chunk)]
+        remote(held, held, ps_sem.at[c, 0], pr_sem.at[c, d], right).wait_recv()
+
+    def pass_on(c, d, gather):
+        heads = [h for h, _ in heads_of(c)]
+        if gather:
+            p_wait(c, d)
+        for h in heads:
+            total = mine[d, h]
+            if gather:
+                total = total + got[d, h].astype(jnp.float32)
+            part[d, h] = total.astype(jnp.bfloat16)
+        pl.when(d <= me)(lambda: p_left(c, d).start())
+        pl.when(d > me)(lambda: p_right(c, d).start())
+
+    chain = far_slots + [n - 1, 1]
+
+    def scores(c):
+        for d in [0, 1, n - 1] + far_slots:
+            if d == 0:
+                x_copy(c, 0).wait_recv()
+                x_copy(c, 1).wait_recv()
+            score_block(c, d)
+            if c + 1 < chunks:
+                if d == 0:
+                    take_queries(c + 1, 1)
+                    take_queries(c + 1, n - 1)
+                elif d == 1:
+                    for far in far_slots:
+                        take_queries(c + 1, far)
+        for d in range(1, n):
+            stats_copy(c, d).start()
+
+    def values(c):
+        x_copy(c, 2).wait_recv()
+        x_copy(c, 3).wait_recv()
+        turn_values(c)
+        for d in range(1, n):
+            stats_copy(c, d).wait_recv()
+        for d in chain:
+            value_block(c, d)
+
+        @pl.when(jnp.logical_not(middle))
+        def _():
+            for d in chain:
+                pass_on(c, d, False)
+
+        value_block(c, 0)
+
+    def combine(c):
+        @pl.when(middle)
+        def _():
+            for d in chain:
+                pass_on(c, d, True)
+
+    def finish(c):
+        pl.when(has_right)(lambda: p_wait(c, 0))
+        pl.when(has_left)(lambda: p_wait(c, n))
+        for h, cut in heads_of(c):
+            total = mine[0, h]
+            total = total + jnp.where(has_right, got[0, h].astype(jnp.float32), 0.0)
+            total = total + jnp.where(has_left, got[n, h].astype(jnp.float32), 0.0)
+            out_ref[:, :, cut] = total.T.reshape(frame_count, row_count, HEAD_DIM).astype(
+                jnp.bfloat16
+            )
+
+    got[0] = jnp.zeros_like(got[0])
+    got[n] = jnp.zeros_like(got[n])
     for copy in loads:
         copy.wait()
-    xcopies[0].wait_recv()
-    xcopies[1].wait_recv()
-    each_head(score_block(0))
-    for d in order[1:]:
+    for d in range(1, n):
         icopies[d].wait_recv()
-        qcopies[d].wait_recv()
-        each_head(score_block(d))
-    scopies = [None] + [
-        remote(stats.at[0], stats.at[d], ss_sem.at[d], sr_sem.at[d], ahead[d])
-        for d in range(1, n)
-    ]
-    for copy in scopies[1:]:
-        copy.start()
-    xcopies[2].wait_recv()
-    xcopies[3].wait_recv()
-    each_head(turn_values)
-    for copy in scopies[1:]:
-        copy.wait_recv()
-    pcopies = [None] + [
-        remote(part.at[d], got.at[d], ps_sem.at[d], pr_sem.at[d], behind[d]) for d in range(1, n)
-    ]
-    for d in order[:0:-1]:
-        each_head(value_block(d))
-        pcopies[d].start()
-    each_head(value_block(0))
-    for copy in pcopies[1:]:
-        copy.wait_recv()
-
-    def finish(h):
-        total = own[h]
+    take_queries(0, 1)
+    take_queries(0, n - 1)
+    for d in far_slots:
+        take_queries(0, d)
+    scores(0)
+    for c in range(chunks):
+        if c + 1 < chunks:
+            scores(c + 1)
+        if c >= 1:
+            combine(c - 1)
+        values(c)
+    combine(chunks - 1)
+    for c in range(chunks):
+        finish(c)
+
+    for copy in icopies[1:]:
+        copy.wait_send()
+    for c in range(chunks):
+        for k in range(4):
+            x_copy(c, k).wait_send()
+        for d in range(n):
+            for flag, make in q_moves(d):
+                pl.when(flag)(lambda make=make: make(c, d).wait_send())
         for d in range(1, n):
-            total = total + got[d, h].astype(jnp.float32)
-        out_ref[:, :, lanes(h)] = total.T.reshape(frame_count, row_count, HEAD_DIM).astype(
-            jnp.bfloat16
-        )
-
-    each_head(finish)
-    for copies in (xcopies, qcopies[1:], icopies[1:], scopies[1:], pcopies[1:]):
-        for copy in copies:
-            copy.wait_send()
+            stats_copy(c, d).wait_send()
+            held = part.at[d, pl.ds(c * per_chunk, per_chunk)]
+            remote(held, held, ps_sem.at[c, d], pr_sem.at[c, d], right).wait_send()
 
 
 def local_kernel(tok_q, tok_kv, ref_kv, ref_ids):
     n = lax.axis_size("frames")
     frame_count, row_count, width = tok_q.shape
     heads = width // HEAD_DIM
+    chunks = heads // 2
     tokens = frame_count * row_count
     images, ref_rows = ref_kv.shape[1:3]
     span = 2 * ref_rows
     dma = pltpu.SemaphoreType.DMA
-    anywhere = pl.BlockSpec(memory_space=pl.ANY)
+    in_hbm = pl.BlockSpec(memory_space=pltpu.HBM)
     return pl.pallas_call(
-        functools.partial(kernel, n),
+        functools.partial(kernel, n, chunks),
         out_shape=jax.ShapeDtypeStruct(tok_q.shape, jnp.bfloat16),
-        in_specs=[anywhere] * 3 + [pl.BlockSpec(memory_space=pltpu.SMEM)],
+        in_specs=[in_hbm] * 3 + [pl.BlockSpec(memory_space=pltpu.SMEM)],
         out_specs=pl.BlockSpec(memory_space=pltpu.VMEM),
         scratch_shapes=[
             pltpu.VMEM((n,) + tok_q.shape, jnp.bfloat16),
@@ -385,18 +483,25 @@
             pltpu.VMEM((n, heads, span, tokens), jnp.float32),
             pltpu.VMEM((n, heads, tokens, tokens), jnp.float32),
             pltpu.VMEM((heads, 2, tokens, tokens), jnp.float32),
-            pltpu.VMEM((n, n, heads, 4, tokens), jnp.float32),
+            pltpu.VMEM((n, chunks, n, heads // chunks, 4, tokens), jnp.float32),
             pltpu.VMEM((heads, HEAD_DIM, images * span + 2 * tokens), jnp.bfloat16),
-            pltpu.VMEM((heads, HEAD_DIM, tokens), jnp.float32),
+            pltpu.VMEM((n, heads, HEAD_DIM, tokens), jnp.float32),
             pltpu.VMEM((n, heads, HEAD_DIM, tokens), jnp.bfloat16),
-            pltpu.VMEM((n, heads, HEAD_DIM, tokens), jnp.bfloat16),
+            pltpu.VMEM((n + 1, heads, HEAD_DIM, tokens), jnp.bfloat16),
             dma((4,)),
-            dma((4,)),
-            dma((4,)),
-        ]
-        + [dma((n,))] * 8,
+            dma((chunks, 4)),
+            dma((chunks, 4)),
+            dma((chunks, n + 1)),
+            dma((chunks, n)),
+            dma((n,)),
+            dma((n,)),
+            dma((chunks, n)),
+            dma((chunks, n)),
+            dma((chunks, n)),
+            dma((chunks, n + 1)),
+        ],
         compiler_params=pltpu.CompilerParams(
-            collective_id=0, has_side_effects=True, vmem_limit_bytes=48 * 1024 * 1024
+            collective_id=0, has_side_effects=True, vmem_limit_bytes=64 * 1024 * 1024
         ),
     )(tok_q, tok_kv, ref_kv, ref_ids)
 
@@ -404,7 +509,7 @@
 def local(tok_q, tok_kv, ref_kv, ref_ids):
     frame_count, row_count, width = tok_q.shape
     fits = (
-        3 <= lax.axis_size("frames") <= 8
+        3 <= lax.axis_size("frames") <= 4
         and lax.axis_size("rows") == 2
         and frame_count == BAND
         and row_count % 16 == 0

time: 51.4 us -> 52.7 us (1.025)
  the two profiles are of different devices: /device:TPU:10 before, /device:TPU:0 now
where the time goes in v2:
time: 52.7 us; the launch traced here: 52.5 us
  Pallas kernels  50.9 us (97%)
  local copies, waits for them, and re-layouts  1.62 us (3%)
    pallas_call x1, Pallas kernels, local_kernel(): pl.pallas_call(functools.partial(kernel, n, chunks), out_shape=jax.ShapeD...  50.9 us
    unnamed x1, local copies, waits for them, and re-layouts  1.62 us

profile of v2, /device:TPU:0, one launch (start us, length us, event | category | flops | bytes accessed | tf_op | source)
XLA Modules:
  0.0 52.5 jit_solution(4589911574574748422)
XLA Ops:
  0.0 50.9 %shard_map.46 = bf16[8,16,768]{2,1,0:T(8,128)(2,1)} custom-call(bf16[8,16,768]{2,1,0:T(8,128)(2,1)} %q_hbm.1, bf16[2,8,16,768]{3,2,1,0:T(8,128)(2,1)} %kv_hbm.1, bf16[2,2,96,768]{3,2,1,0:T(8,128)(2,1)} %ref_hbm.1, s32[8]{0:T(128)} %ids_ref.1), custom_call_target="tpu_custom_call" | custom-call | tf_op jit(solution)/shard_map/pallas_call | solution.py:473
  50.9 1.6 %copy.6 = bf16[8,16,768]{2,1,0:T(8,128)(2,1)} copy(bf16[8,16,768]{2,1,0:T(8,128)(2,1)} %shard_map.46) | data formatting | bytes 393216

commit v3 on v2

--- a/solution.py
+++ b/solution.py
@@ -240,62 +240,87 @@
         for k in range(4):
             x_copy(c, k).start()
 
-    row = lax.broadcasted_iota(jnp.int32, (tokens, tokens), 0)
-    col = lax.broadcasted_iota(jnp.int32, (tokens, tokens), 1)
-    key_frame, key_row = row // row_count, row % row_count
-    query_frame, query_row = col // row_count, col % row_count
-
-    def in_band(d):
-        mask = key_row == query_row
-        if d == 1:
-            mask = mask & (key_frame <= query_frame)
-        elif d == n - 1:
-            mask = mask & (key_frame >= query_frame)
-        return mask
+    slots = [n - 1, 0, 1] + far_slots
+    banded_width, all_width = 3 * tokens, n * tokens
+    here = slice(tokens, 2 * tokens)
+
+    def grid(width, axis):
+        return lax.broadcasted_iota(jnp.int32, (frame_count, row_count, width), axis)
+
+    def same_row(width):
+        return grid(width, 1) == grid(width, 2) % row_count
+
+    def same_frame():
+        return grid(tokens, 0) == grid(tokens, 2) // row_count
+
+    def in_band():
+        keys = lax.broadcasted_iota(jnp.int32, (frame_count, banded_width), 0)
+        lane = lax.broadcasted_iota(jnp.int32, (frame_count, banded_width), 1)
+        block, frame = lane // tokens, lane % tokens // row_count
+        return (
+            ((block == 0) & (keys >= frame)) | (block == 1) | ((block == 2) & (keys <= frame))
+        )
 
     def heads_of(c):
         return [(h, pl.ds(h * HEAD_DIM, HEAD_DIM)) for h in range(c * per_chunk, (c + 1) * per_chunk)]
 
-    def score_block(c, d):
+    def side_by_side(rows):
+        return jnp.concatenate(rows, axis=1)
+
+    def score_block(c):
+        chosen = side_by_side([idbuf[d][0:1] for d in slots])
         for h, cut in heads_of(c):
-            query = qbuf[d, :, :, cut].reshape(tokens, HEAD_DIM)
+            query = jnp.concatenate(
+                [qbuf[d, :, :, cut].reshape(tokens, HEAD_DIM) for d in slots], axis=0
+            )
             image_keys = rbuf[0, :, :, cut].reshape(images * span, HEAD_DIM)
             both = scores_of(image_keys, query)
-            chosen = idbuf[d][0:1]
             score = both[0:span]
             for i in range(1, images):
                 score = jnp.where(chosen == i, both[i * span : (i + 1) * span], score)
             score = score * factor
+            keys = kvbuf[0, 0, :, :, cut].reshape(tokens, HEAD_DIM)
+            near = scores_of(keys, query[0:banded_width]) * factor
+            near = near.reshape(frame_count, row_count, banded_width)
+            time = jnp.sum(jnp.where(same_row(banded_width), near, 0.0), axis=1)
+            time = jnp.where(in_band(), time, NEG)
+            time_top = jnp.max(time, axis=0, keepdims=True)
+            time = jnp.exp(time - time_top)
+            ptime[h] = time
+            time_sum = jnp.sum(time, axis=0, keepdims=True)
+            other_keys = kvbuf[1, 0, :, :, cut].reshape(tokens, HEAD_DIM)
+            other = scores_of(other_keys, query[here]) * factor
+            other = other.reshape(frame_count, row_count, tokens)
+            frame = jnp.concatenate(
+                [
+                    jnp.sum(jnp.where(same_frame(), near[:, :, here], 0.0), axis=0),
+                    jnp.sum(jnp.where(same_frame(), other, 0.0), axis=0),
+                ],
+                axis=0,
+            )
             top = jnp.max(score, axis=0, keepdims=True)
-            time_top, time_sum = jnp.zeros_like(top), jnp.zeros_like(top)
-            if d in banded:
-                keys = kvbuf[0, 0, :, :, cut].reshape(tokens, HEAD_DIM)
-                near = scores_of(keys, query) * factor
-                time_score = jnp.where(in_band(d), near, NEG)
-                time_top = jnp.max(time_score, axis=0, keepdims=True)
-                time_exp = jnp.exp(time_score - time_top)
-                time_sum = jnp.sum(time_exp, axis=0, keepdims=True)
-                ptime[d, h] = time_exp
-            if d == 0:
-                other_keys = kvbuf[1, 0, :, :, cut].reshape(tokens, HEAD_DIM)
-                other = scores_of(other_keys, query) * factor
-                near = jnp.where(key_frame == query_frame, near, NEG)
-                other = jnp.where(key_frame == query_frame, other, NEG)
-                top = jnp.maximum(top, jnp.max(near, axis=0, keepdims=True))
-                top = jnp.maximum(top, jnp.max(other, axis=0, keepdims=True))
-                near = jnp.exp(near - top)
-                other = jnp.exp(other - top)
-                pframe[h, 0] = near
-                pframe[h, 1] = other
+            frame_top = jnp.max(frame, axis=0, keepdims=True)
+            top = side_by_side(
+                [
+                    top[:, 0:tokens],
+                    jnp.maximum(top[:, here], frame_top),
+                    top[:, 2 * tokens :],
+                ]
+            )
+            frame = jnp.exp(frame - top[:, here])
+            pframe[h] = frame
+            frame_sum = jnp.sum(frame, axis=0, keepdims=True)
             score = jnp.exp(score - top)
+            pref[h] = score
             total = jnp.sum(score, axis=0, keepdims=True)
-            if d == 0:
-                total = total + jnp.sum(near, axis=0, keepdims=True)
-                total = total + jnp.sum(other, axis=0, keepdims=True)
-            pref[d, h] = score
-            stats[0, c, d, h % per_chunk] = jnp.concatenate(
-                [top, total, time_top, time_sum], axis=0
-            )
+            for i, d in enumerate(slots):
+                at = slice(i * tokens, (i + 1) * tokens)
+                rows = [top[:, at], total[:, at] + frame_sum if d == 0 else total[:, at]]
+                if d in banded:
+                    rows += [time_top[:, at], time_sum[:, at]]
+                else:
+                    rows += [jnp.zeros((2, tokens), jnp.float32)]
+                stats[0, c, d, h % per_chunk] = jnp.concatenate(rows, axis=0)
 
     def scale_of(c, d, h, k):
         tops, sums = [], []
@@ -310,28 +335,43 @@
         total = sum(s * jnp.exp(t - top) for t, s in zip(tops, sums))
         return jnp.exp(tops[0] - top) / total
 
-    def value_block(c, d):
+    def value_block(c):
+        chosen = side_by_side([idbuf[d][0:1] for d in slots])
         for h, cut in heads_of(c):
-            chosen = idbuf[d][0:1]
-            scale = scale_of(c, d, h, 0)
-            weight = pref[d, h] * scale
-            weights = [
-                jnp.where(chosen == i, weight, 0.0).astype(jnp.bfloat16) for i in range(images)
+            scale = side_by_side([scale_of(c, d, h, 0) for d in slots])
+            weight = pref[h] * scale
+            weight = jnp.concatenate(
+                [jnp.where(chosen == i, weight, 0.0).astype(jnp.bfloat16) for i in range(images)],
+                axis=0,
+            )
+            start = images * span
+            result = jnp.dot(vt[h, :, 0:start], weight, preferred_element_type=jnp.float32)
+            time = ptime[h] * side_by_side([scale_of(c, d, h, 2) for d in slots[:3]])
+            time = jnp.where(same_row(banded_width), time[:, None, :], 0.0)
+            time = time.reshape(tokens, banded_width).astype(jnp.bfloat16)
+            timed = jnp.dot(
+                vt[h, :, start : start + tokens], time, preferred_element_type=jnp.float32
+            )
+            frame = pframe[h] * scale[:, here]
+            frames = [
+                jnp.where(same_frame(), frame[i * row_count : (i + 1) * row_count][None], 0.0)
+                .reshape(tokens, tokens)
+                .astype(jnp.bfloat16)
+                for i in range(2)
             ]
-            if d in banded:
-                weights.append((ptime[d, h] * scale_of(c, d, h, 2)).astype(jnp.bfloat16))
-            weight = jnp.concatenate(weights, axis=0)
-            values = vt[h, :, 0 : weight.shape[0]]
-            result = jnp.dot(values, weight, preferred_element_type=jnp.float32)
-            if d == 0:
-                for i in range(2):
-                    start = images * span + i * tokens
-                    result = result + jnp.dot(
-                        vt[h, :, start : start + tokens],
-                        (pframe[h, i] * scale).astype(jnp.bfloat16),
-                        preferred_element_type=jnp.float32,
-                    )
-            mine[d, h] = result
+            framed = jnp.dot(
+                vt[h, :, start : start + 2 * tokens],
+                jnp.concatenate(frames, axis=0),
+                preferred_element_type=jnp.float32,
+            )
+            for i, d in enumerate(slots):
+                at = slice(i * tokens, (i + 1) * tokens)
+                piece = result[:, at]
+                if d in banded:
+                    piece = piece + timed[:, at]
+                if d == 0:
+                    piece = piece + framed
+                mine[d, h] = piece
 
     def turn_values(c):
         for h, cut in heads_of(c):
@@ -377,18 +417,11 @@
     chain = far_slots + [n - 1, 1]
 
     def scores(c):
-        for d in [0, 1, n - 1] + far_slots:
-            if d == 0:
-                x_copy(c, 0).wait_recv()
-                x_copy(c, 1).wait_recv()
-            score_block(c, d)
-            if c + 1 < chunks:
-                if d == 0:
-                    take_queries(c + 1, 1)
-                    take_queries(c + 1, n - 1)
-                elif d == 1:
-                    for far in far_slots:
-                        take_queries(c + 1, far)
+        for d in [1, n - 1] + far_slots:
+            take_queries(c, d)
+        x_copy(c, 0).wait_recv()
+        x_copy(c, 1).wait_recv()
+        score_block(c)
         for d in range(1, n):
             stats_copy(c, d).start()
 
@@ -398,15 +431,12 @@
         turn_values(c)
         for d in range(1, n):
             stats_copy(c, d).wait_recv()
-        for d in chain:
-            value_block(c, d)
+        value_block(c)
 
         @pl.when(jnp.logical_not(middle))
         def _():
             for d in chain:
                 pass_on(c, d, False)
-
-        value_block(c, 0)
 
     def combine(c):
         @pl.when(middle)
@@ -431,10 +461,6 @@
         copy.wait()
     for d in range(1, n):
         icopies[d].wait_recv()
-    take_queries(0, 1)
-    take_queries(0, n - 1)
-    for d in far_slots:
-        take_queries(0, d)
     scores(0)
     for c in range(chunks):
         if c + 1 < chunks:
@@ -480,9 +506,9 @@
             pltpu.VMEM((2,) + tok_kv.shape, jnp.bfloat16),
             pltpu.VMEM((2, images, span, width), jnp.bfloat16),
             pltpu.VMEM((n, 8, tokens), jnp.int32),
-            pltpu.VMEM((n, heads, span, tokens), jnp.float32),
-            pltpu.VMEM((n, heads, tokens, tokens), jnp.float32),
-            pltpu.VMEM((heads, 2, tokens, tokens), jnp.float32),
+            pltpu.VMEM((heads, span, n * tokens), jnp.float32),
+            pltpu.VMEM((heads, frame_count, 3 * tokens), jnp.float32),
+            pltpu.VMEM((heads, 2 * row_count, tokens), jnp.float32),
             pltpu.VMEM((n, chunks, n, heads // chunks, 4, tokens), jnp.float32),
             pltpu.VMEM((heads, HEAD_DIM, images * span + 2 * tokens), jnp.bfloat16),
             pltpu.VMEM((n, heads, HEAD_DIM, tokens), jnp.float32),

time: 52.7 us -> 49.3 us (0.935)
  Pallas kernels: 50.9 us -> 47.5 us
    pallas_call x1, Pallas kernels: 50.9 us -> 47.5 us  [local_kernel(): pl.pallas_call(functools.partial(kernel, n, chunks), out_shape=jax.ShapeD...]
where the time goes in v3:
time: 49.3 us; the launch traced here: 49.2 us
  Pallas kernels  47.5 us (96%)
  local copies, waits for them, and re-layouts  1.62 us (3%)
    pallas_call x1, Pallas kernels, local_kernel(): pl.pallas_call(functools.partial(kernel, n, chunks), out_shape=jax.ShapeD...  47.5 us
    unnamed x1, local copies, waits for them, and re-layouts  1.62 us

profile of v3, /device:TPU:0, one launch (start us, length us, event | category | flops | bytes accessed | tf_op | source)
XLA Modules:
  0.0 49.2 jit_solution(1972903816418779001)
XLA Ops:
  0.0 47.5 %shard_map.46 = bf16[8,16,768]{2,1,0:T(8,128)(2,1)} custom-call(bf16[8,16,768]{2,1,0:T(8,128)(2,1)} %q_hbm.1, bf16[2,8,16,768]{3,2,1,0:T(8,128)(2,1)} %kv_hbm.1, bf16[2,2,96,768]{3,2,1,0:T(8,128)(2,1)} %ref_hbm.1, s32[8]{0:T(128)} %ids_ref.1), custom_call_target="tpu_custom_call" | custom-call | tf_op jit(solution)/shard_map/pallas_call | solution.py:499
  47.5 1.6 %copy.6 = bf16[8,16,768]{2,1,0:T(8,128)(2,1)} copy(bf16[8,16,768]{2,1,0:T(8,128)(2,1)} %shard_map.46) | data formatting | bytes 393216

commit v4 on v3

--- a/solution.py
+++ b/solution.py
@@ -195,6 +195,16 @@
             src, dst = kv_hbm.at[k // 2, :, :, cut], kvbuf.at[1, k // 2, :, :, cut]
         return remote(src, dst, xs_sem.at[c, k], xr_sem.at[c, k], across)
 
+    def x_keys(c):
+        if c < chunks:
+            x_copy(c, 0).start()
+            x_copy(c, 1).start()
+
+    def x_values(c):
+        if c < chunks:
+            x_copy(c, 2).start()
+            x_copy(c, 3).start()
+
     def q_right(c, d):
         cut = part_of(c)
         src = q_hbm.at[:, :, cut] if d == 0 else qbuf.at[d, :, :, cut]
@@ -235,10 +245,11 @@
     ]
     for copy in icopies[1:]:
         copy.start()
-    for c in range(chunks):
+    send_queries(0, 0)
+    x_keys(0)
+    for c in range(1, chunks):
         send_queries(c, 0)
-        for k in range(4):
-            x_copy(c, k).start()
+    x_values(0)
 
     slots = [n - 1, 0, 1] + far_slots
     banded_width, all_width = 3 * tokens, n * tokens
@@ -416,9 +427,17 @@
 
     chain = far_slots + [n - 1, 1]
 
+    def take_near(c):
+        if c < chunks:
+            take_queries(c, 1)
+            take_queries(c, n - 1)
+
+    def take_far(c):
+        if c < chunks:
+            for d in far_slots:
+                take_queries(c, d)
+
     def scores(c):
-        for d in [1, n - 1] + far_slots:
-            take_queries(c, d)
         x_copy(c, 0).wait_recv()
         x_copy(c, 1).wait_recv()
         score_block(c)
@@ -461,13 +480,24 @@
         copy.wait()
     for d in range(1, n):
         icopies[d].wait_recv()
-    scores(0)
+    take_near(0)
+    x_keys(1)
+    take_far(0)
+    take_near(1)
+    x_values(1)
     for c in range(chunks):
-        if c + 1 < chunks:
-            scores(c + 1)
+        scores(c)
+        take_far(c + 1)
+        take_near(c + 2)
+        x_keys(c + 2)
+        x_values(c + 2)
+        if c >= 2:
+            combine(c - 2)
         if c >= 1:
-            combine(c - 1)
-        values(c)
+            values(c - 1)
+    if chunks >= 2:
+        combine(chunks - 2)
+    values(chunks - 1)
     combine(chunks - 1)
     for c in range(chunks):
         finish(c)

time: 49.3 us -> 52 us (1.055)
  Pallas kernels: 47.5 us -> 50.2 us
    pallas_call x1, Pallas kernels: 47.5 us -> 50.2 us  [local_kernel(): pl.pallas_call(functools.partial(kernel, n, chunks), out_shape=jax.ShapeD...]
where the time goes in v4:
time: 52 us; the launch traced here: 51.8 us
  Pallas kernels  50.2 us (97%)
  local copies, waits for them, and re-layouts  1.62 us (3%)
    pallas_call x1, Pallas kernels, local_kernel(): pl.pallas_call(functools.partial(kernel, n, chunks), out_shape=jax.ShapeD...  50.2 us
    unnamed x1, local copies, waits for them, and re-layouts  1.62 us

profile of v4, /device:TPU:0, one launch (start us, length us, event | category | flops | bytes accessed | tf_op | source)
XLA Modules:
  0.0 51.8 jit_solution(17690122129600512223)
XLA Ops:
  0.0 50.2 %shard_map.46 = bf16[8,16,768]{2,1,0:T(8,128)(2,1)} custom-call(bf16[8,16,768]{2,1,0:T(8,128)(2,1)} %q_hbm.1, bf16[2,8,16,768]{3,2,1,0:T(8,128)(2,1)} %kv_hbm.1, bf16[2,2,96,768]{3,2,1,0:T(8,128)(2,1)} %ref_hbm.1, s32[8]{0:T(128)} %ids_ref.1), custom_call_target="tpu_custom_call" | custom-call | tf_op jit(solution)/shard_map/pallas_call | solution.py:529
  50.2 1.6 %copy.6 = bf16[8,16,768]{2,1,0:T(8,128)(2,1)} copy(bf16[8,16,768]{2,1,0:T(8,128)(2,1)} %shard_map.46) | data formatting | bytes 393216

commit v5 on v3

--- a/solution.py
+++ b/solution.py
@@ -247,19 +247,21 @@
     def grid(width, axis):
         return lax.broadcasted_iota(jnp.int32, (frame_count, row_count, width), axis)
 
+    lane = lax.broadcasted_iota(jnp.int32, (1, banded_width), 1)
+    lane_row, lane_block = lax.rem(lane, row_count), lax.div(lane, tokens)
+    band_frame = lax.div(lax.rem(lane, tokens), row_count)
+    lane_low = jnp.where(lane_block == 0, band_frame, 0)
+    lane_high = jnp.where(lane_block == 2, band_frame, frame_count)
+
     def same_row(width):
-        return grid(width, 1) == grid(width, 2) % row_count
+        return grid(width, 1) == lane_row[None]
 
     def same_frame():
-        return grid(tokens, 0) == grid(tokens, 2) // row_count
+        return grid(tokens, 0) == band_frame[None, :, here]
 
     def in_band():
         keys = lax.broadcasted_iota(jnp.int32, (frame_count, banded_width), 0)
-        lane = lax.broadcasted_iota(jnp.int32, (frame_count, banded_width), 1)
-        block, frame = lane // tokens, lane % tokens // row_count
-        return (
-            ((block == 0) & (keys >= frame)) | (block == 1) | ((block == 2) & (keys <= frame))
-        )
+        return (keys >= lane_low) & (keys <= lane_high)
 
     def heads_of(c):
         return [(h, pl.ds(h * HEAD_DIM, HEAD_DIM)) for h in range(c * per_chunk, (c + 1) * per_chunk)]

time: 49.3 us -> 49.3 us (level)
  no operation moved by 1% of the time
where the time goes in v5:
time: 49.3 us; the launch traced here: 49.2 us
  Pallas kernels  47.6 us (97%)
  local copies, waits for them, and re-layouts  1.62 us (3%)
    pallas_call x1, Pallas kernels, local_kernel(): pl.pallas_call(functools.partial(kernel, n, chunks), out_shape=jax.ShapeD...  47.6 us
    unnamed x1, local copies, waits for them, and re-layouts  1.62 us

profile of v5, /device:TPU:0, one launch (start us, length us, event | category | flops | bytes accessed | tf_op | source)
XLA Modules:
  0.0 49.2 jit_solution(10055707809478498214)
XLA Ops:
  0.0 47.6 %shard_map.46 = bf16[8,16,768]{2,1,0:T(8,128)(2,1)} custom-call(bf16[8,16,768]{2,1,0:T(8,128)(2,1)} %q_hbm.1, bf16[2,8,16,768]{3,2,1,0:T(8,128)(2,1)} %kv_hbm.1, bf16[2,2,96,768]{3,2,1,0:T(8,128)(2,1)} %ref_hbm.1, s32[8]{0:T(128)} %ids_ref.1), custom_call_target="tpu_custom_call" | custom-call | tf_op jit(solution)/shard_map/pallas_call | solution.py:501
  47.6 1.6 %copy.6 = bf16[8,16,768]{2,1,0:T(8,128)(2,1)} copy(bf16[8,16,768]{2,1,0:T(8,128)(2,1)} %shard_map.46) | data formatting | bytes 393216

commit v6 on v5

--- a/solution.py
+++ b/solution.py
@@ -109,6 +109,7 @@
 def kernel(
     n,
     chunks,
+    pieces,
     q_hbm,
     kv_hbm,
     ref_hbm,
@@ -141,7 +142,6 @@
     frame_count, row_count, width = q_hbm.shape
     head_count = width // HEAD_DIM
     per_chunk = head_count // chunks
-    chunk_width = per_chunk * HEAD_DIM
     tokens = frame_count * row_count
     images, ref_rows = ref_hbm.shape[1], ref_hbm.shape[2]
     span = 2 * ref_rows
@@ -184,30 +184,28 @@
             device_id=where, device_id_type=MESH,
         )
 
-    def part_of(c):
-        return pl.ds(c * chunk_width, chunk_width)
-
-    def x_copy(c, k):
-        cut = part_of(c)
+    def x_copy(k):
         if k % 2 == 0:
-            src, dst = ref_hbm.at[k // 2, :, :, cut], rbuf.at[k // 2, :, far_rows, cut]
+            src, dst = ref_hbm.at[k // 2], rbuf.at[k // 2, :, far_rows]
         else:
-            src, dst = kv_hbm.at[k // 2, :, :, cut], kvbuf.at[1, k // 2, :, :, cut]
-        return remote(src, dst, xs_sem.at[c, k], xr_sem.at[c, k], across)
-
-    def q_right(c, d):
-        cut = part_of(c)
-        src = q_hbm.at[:, :, cut] if d == 0 else qbuf.at[d, :, :, cut]
-        return remote(
-            src, qbuf.at[d + 1, :, :, cut], qs_sem.at[c, d], qr_sem.at[c, d + 1], right
-        )
-
-    def q_left(c, d):
-        cut = part_of(c)
-        src = q_hbm.at[:, :, cut] if d == 0 else qbuf.at[d, :, :, cut]
+            src, dst = kv_hbm.at[k // 2], kvbuf.at[1, k // 2]
+        return remote(src, dst, xs_sem.at[k], xr_sem.at[k], across)
+
+    def piece(p):
+        count = frame_count // pieces
+        return pl.ds(p * count, count)
+
+    def q_right(p, d):
+        cut = piece(p)
+        src = q_hbm.at[cut] if d == 0 else qbuf.at[d, cut]
+        return remote(src, qbuf.at[d + 1, cut], qs_sem.at[p, d], qr_sem.at[p, d + 1], right)
+
+    def q_left(p, d):
+        cut = piece(p)
+        src = q_hbm.at[cut] if d == 0 else qbuf.at[d, cut]
         to = (d if d else n) - 1
         return remote(
-            src, qbuf.at[to, :, :, cut], qs_sem.at[c, d if d else n], qr_sem.at[c, to], left
+            src, qbuf.at[to, cut], qs_sem.at[p, d if d else n], qr_sem.at[p, to], left
         )
 
     def q_moves(d):
@@ -220,25 +218,25 @@
             moves.append(((d > me) & has_left, q_left))
         return moves
 
-    def send_queries(c, d):
+    def send_queries(p, d):
         for flag, make in q_moves(d):
-            pl.when(flag)(lambda make=make: make(c, d).start())
-
-    def take_queries(c, d):
-        cut = part_of(c)
-        held = qbuf.at[d, :, :, cut]
-        remote(held, held, qs_sem.at[c, d], qr_sem.at[c, d], right).wait_recv()
-        send_queries(c, d)
+            pl.when(flag)(lambda make=make: make(p, d).start())
+
+    def take_queries(p, d):
+        held = qbuf.at[d, piece(p)]
+        remote(held, held, qs_sem.at[p, d], qr_sem.at[p, d], right).wait_recv()
+        send_queries(p, d)
 
     icopies = [None] + [
         remote(idbuf.at[0], idbuf.at[d], is_sem.at[d], ir_sem.at[d], ahead[d]) for d in range(1, n)
     ]
     for copy in icopies[1:]:
         copy.start()
-    for c in range(chunks):
-        send_queries(c, 0)
-        for k in range(4):
-            x_copy(c, k).start()
+    x_copy(0).start()
+    for p in range(pieces):
+        send_queries(p, 0)
+    for k in range(1, 4):
+        x_copy(k).start()
 
     slots = [n - 1, 0, 1] + far_slots
     banded_width, all_width = 3 * tokens, n * tokens
@@ -419,17 +417,11 @@
     chain = far_slots + [n - 1, 1]
 
     def scores(c):
-        for d in [1, n - 1] + far_slots:
-            take_queries(c, d)
-        x_copy(c, 0).wait_recv()
-        x_copy(c, 1).wait_recv()
         score_block(c)
         for d in range(1, n):
             stats_copy(c, d).start()
 
     def values(c):
-        x_copy(c, 2).wait_recv()
-        x_copy(c, 3).wait_recv()
         turn_values(c)
         for d in range(1, n):
             stats_copy(c, d).wait_recv()
@@ -463,25 +455,33 @@
         copy.wait()
     for d in range(1, n):
         icopies[d].wait_recv()
-    scores(0)
+    for group in ([1, n - 1], far_slots):
+        for p in range(pieces):
+            for d in group:
+                take_queries(p, d)
+    x_copy(0).wait_recv()
+    x_copy(1).wait_recv()
     for c in range(chunks):
-        if c + 1 < chunks:
-            scores(c + 1)
+        scores(c)
+    x_copy(2).wait_recv()
+    x_copy(3).wait_recv()
+    for c in range(chunks):
+        values(c)
         if c >= 1:
             combine(c - 1)
-        values(c)
     combine(chunks - 1)
     for c in range(chunks):
         finish(c)
 
     for copy in icopies[1:]:
         copy.wait_send()
-    for c in range(chunks):
-        for k in range(4):
-            x_copy(c, k).wait_send()
+    for k in range(4):
+        x_copy(k).wait_send()
+    for p in range(pieces):
         for d in range(n):
             for flag, make in q_moves(d):
-                pl.when(flag)(lambda make=make: make(c, d).wait_send())
+                pl.when(flag)(lambda make=make: make(p, d).wait_send())
+    for c in range(chunks):
         for d in range(1, n):
             stats_copy(c, d).wait_send()
             held = part.at[d, pl.ds(c * per_chunk, per_chunk)]
@@ -492,14 +492,14 @@
     n = lax.axis_size("frames")
     frame_count, row_count, width = tok_q.shape
     heads = width // HEAD_DIM
-    chunks = heads // 2
+    chunks, pieces = heads // 2, 2
     tokens = frame_count * row_count
     images, ref_rows = ref_kv.shape[1:3]
     span = 2 * ref_rows
     dma = pltpu.SemaphoreType.DMA
     in_hbm = pl.BlockSpec(memory_space=pltpu.HBM)
     return pl.pallas_call(
-        functools.partial(kernel, n, chunks),
+        functools.partial(kernel, n, chunks, pieces),
         out_shape=jax.ShapeDtypeStruct(tok_q.shape, jnp.bfloat16),
         in_specs=[in_hbm] * 3 + [pl.BlockSpec(memory_space=pltpu.SMEM)],
         out_specs=pl.BlockSpec(memory_space=pltpu.VMEM),
@@ -517,10 +517,10 @@
             pltpu.VMEM((n, heads, HEAD_DIM, tokens), jnp.bfloat16),
             pltpu.VMEM((n + 1, heads, HEAD_DIM, tokens), jnp.bfloat16),
             dma((4,)),
-            dma((chunks, 4)),
-            dma((chunks, 4)),
-            dma((chunks, n + 1)),
-            dma((chunks, n)),
+            dma((4,)),
+            dma((4,)),
+            dma((pieces, n + 1)),
+            dma((pieces, n)),
             dma((n,)),
             dma((n,)),
             dma((chunks, n)),

time: 49.3 us -> 55.4 us (1.12)
  Pallas kernels: 47.6 us -> 53.6 us
    pallas_call x1, Pallas kernels: 47.6 us -> 53.6 us  [local_kernel(): pl.pallas_call(functools.partial(kernel, n, chunks, pieces), out_shape=ja...]
where the time goes in v6:
time: 55.4 us; the launch traced here: 55.2 us
  Pallas kernels  53.6 us (97%)
  local copies, waits for them, and re-layouts  1.62 us (3%)
    pallas_call x1, Pallas kernels, local_kernel(): pl.pallas_call(functools.partial(kernel, n, chunks, pieces), out_shape=ja...  53.6 us
    unnamed x1, local copies, waits for them, and re-layouts  1.62 us

profile of v6, /device:TPU:0, one launch (start us, length us, event | category | flops | bytes accessed | tf_op | source)
XLA Modules:
  0.0 55.2 jit_solution(14581695989682150316)
XLA Ops:
  0.0 53.6 %shard_map.46 = bf16[8,16,768]{2,1,0:T(8,128)(2,1)} custom-call(bf16[8,16,768]{2,1,0:T(8,128)(2,1)} %q_hbm.1, bf16[2,8,16,768]{3,2,1,0:T(8,128)(2,1)} %kv_hbm.1, bf16[2,2,96,768]{3,2,1,0:T(8,128)(2,1)} %ref_hbm.1, s32[8]{0:T(128)} %ids_ref.1), custom_call_target="tpu_custom_call" | custom-call | tf_op jit(solution)/shard_map/pallas_call | solution.py:501
  53.6 1.6 %copy.6 = bf16[8,16,768]{2,1,0:T(8,128)(2,1)} copy(bf16[8,16,768]{2,1,0:T(8,128)(2,1)} %shard_map.46) | data formatting | bytes 393216

commit v7 on v5

--- a/solution.py
+++ b/solution.py
@@ -176,6 +176,8 @@
         which = jnp.where(lane_frame == f, ids_ref[f], which)
     idbuf[0] = which
 
+    for copy in loads:
+        copy.wait()
     pl.semaphore_wait(barrier, n)
 
     def remote(src, dst, send, recv, where):
@@ -190,21 +192,21 @@
     def x_copy(c, k):
         cut = part_of(c)
         if k % 2 == 0:
-            src, dst = ref_hbm.at[k // 2, :, :, cut], rbuf.at[k // 2, :, far_rows, cut]
+            src, dst = rbuf.at[k // 2, :, own_rows, cut], rbuf.at[k // 2, :, far_rows, cut]
         else:
-            src, dst = kv_hbm.at[k // 2, :, :, cut], kvbuf.at[1, k // 2, :, :, cut]
+            src, dst = kvbuf.at[0, k // 2, :, :, cut], kvbuf.at[1, k // 2, :, :, cut]
         return remote(src, dst, xs_sem.at[c, k], xr_sem.at[c, k], across)
 
     def q_right(c, d):
         cut = part_of(c)
-        src = q_hbm.at[:, :, cut] if d == 0 else qbuf.at[d, :, :, cut]
+        src = qbuf.at[d, :, :, cut]
         return remote(
             src, qbuf.at[d + 1, :, :, cut], qs_sem.at[c, d], qr_sem.at[c, d + 1], right
         )
 
     def q_left(c, d):
         cut = part_of(c)
-        src = q_hbm.at[:, :, cut] if d == 0 else qbuf.at[d, :, :, cut]
+        src = qbuf.at[d, :, :, cut]
         to = (d if d else n) - 1
         return remote(
             src, qbuf.at[to, :, :, cut], qs_sem.at[c, d if d else n], qr_sem.at[c, to], left
@@ -459,8 +461,6 @@
 
     got[0] = jnp.zeros_like(got[0])
     got[n] = jnp.zeros_like(got[n])
-    for copy in loads:
-        copy.wait()
     for d in range(1, n):
         icopies[d].wait_recv()
     scores(0)

time: 49.3 us -> 49.1 us (level)
  no operation moved by 1% of the time
where the time goes in v7:
time: 49.1 us; the launch traced here: 48.9 us
  Pallas kernels  47.3 us (96%)
  local copies, waits for them, and re-layouts  1.62 us (3%)
    pallas_call x1, Pallas kernels, local_kernel(): pl.pallas_call(functools.partial(kernel, n, chunks), out_shape=jax.ShapeD...  47.3 us
    unnamed x1, local copies, waits for them, and re-layouts  1.62 us

profile of v7, /device:TPU:0, one launch (start us, length us, event | category | flops | bytes accessed | tf_op | source)
XLA Modules:
  0.0 48.9 jit_solution(12765659821878548978)
XLA Ops:
  0.0 47.3 %shard_map.46 = bf16[8,16,768]{2,1,0:T(8,128)(2,1)} custom-call(bf16[8,16,768]{2,1,0:T(8,128)(2,1)} %q_hbm.1, bf16[2,8,16,768]{3,2,1,0:T(8,128)(2,1)} %kv_hbm.1, bf16[2,2,96,768]{3,2,1,0:T(8,128)(2,1)} %ref_hbm.1, s32[8]{0:T(128)} %ids_ref.1), custom_call_target="tpu_custom_call" | custom-call | tf_op jit(solution)/shard_map/pallas_call | solution.py:501
  47.3 1.6 %copy.6 = bf16[8,16,768]{2,1,0:T(8,128)(2,1)} copy(bf16[8,16,768]{2,1,0:T(8,128)(2,1)} %shard_map.46) | data formatting | bytes 393216
